TPU v7x, 256 devices: a whole 4x4x8 slice. The times are simulated.
256 devices in a mesh: col: 32 (over z_hi, x, core), row: 8 (over z_lo, y).
Axes of the slice: x: 4, y: 4, z: 8 (z_hi: 4, z_lo: 2; z = z_hi * 2 + z_lo), core: 2. Of those that a mesh axis runs over, the one named last changes fastest.
Arguments:
- row_vecs: bfloat16 [32768, 300], P(('row', 'col')), may hold values from -0.8984375 to 0.8984375
- row_bias: bfloat16 [32768], P(('row', 'col')), may hold values from -4 to 4
- col_vecs: bfloat16 [204800, 300], P(('col', 'row')), may hold values from -0.8984375 to 0.8984375
- col_bias: bfloat16 [204800], P(('col', 'row')), may hold values from -4 to 4
- row_block: int32 [8, 32, 128], P('row', 'col'), may hold values from 0 to 31, as said below
- col_block: int32 [8, 32, 128], P('row', 'col'), may hold values from 0 to 49
- counts: int32 [8, 32, 128, 128, 128], P('row', 'col'), may hold values from 0 to 512, as said below
- block_totals: int32 [8, 32], replicated, may hold values from 42 to 128, as said below
Outputs:
- grad_rows: float32 [32768, 300], P(('row', 'col'))
- grad_row_bias: float32 [32768], P(('row', 'col'))
- grad_cols: float32 [204800, 300], P(('col', 'row'))
- grad_col_bias: float32 [204800], P(('col', 'row'))
Inputs may be any that keep to these rules, and one draw needn't show every extreme that they name: On each device the pairs (row_block, col_block) of its 128 slots are distinct. Slots at or after a device's block total may hold any counts. `block_totals`: some device has exactly 128 live slots and some other device exactly 42.
All inputs are finite; a program needn't handle non-finite values.
Results may differ from a plain program's by a relative error of at most 0.0028.
Values may be sent and summed in bfloat16 or wider, within the bound.
A program may use at most 192 MiB of HBM per device.

v0:
```python
import jax
import jax.numpy as jnp
from jax import lax
from jax.sharding import PartitionSpec as P


def block_grads(count_tiles, row_part, col_part, row_shift, col_shift, live_mask):
    counts_real = count_tiles.astype(jnp.float32)
    scores = jnp.einsum("nid,njd->nij", row_part, col_part, preferred_element_type=jnp.float32)
    residual = (
        scores
        + row_shift.astype(jnp.float32)[:, :, None]
        + col_shift.astype(jnp.float32)[:, None, :]
        - jnp.log(jnp.maximum(counts_real, 1.0))
    )
    weights = jnp.minimum(1.0, jnp.power(counts_real / 100.0, 0.75))
    terms = 2.0 * weights * residual * live_mask[:, None, None]
    rounded = terms.astype(jnp.bfloat16)
    grad_rows = jnp.einsum("nij,njd->nid", rounded, col_part, preferred_element_type=jnp.float32)
    grad_cols = jnp.einsum("nij,nid->njd", rounded, row_part, preferred_element_type=jnp.float32)
    return (grad_rows, grad_cols, jnp.sum(terms, axis=2), jnp.sum(terms, axis=1))


def accumulate(partials, row_pick, col_pick, pieces):
    return (
        partials[0].at[row_pick].add(pieces[0]),
        partials[1].at[col_pick].add(pieces[1]),
        partials[2].at[row_pick].add(pieces[2]),
        partials[3].at[col_pick].add(pieces[3]),
    )


def body(row_vecs, row_bias, col_vecs, col_bias, row_block, col_block, counts, block_totals):
    row_full, row_shift_full = (
        lax.all_gather(row_vecs, "col", axis=0, tiled=True),
        lax.all_gather(row_bias, "col", axis=0, tiled=True),
    )
    col_full, col_shift_full = (
        lax.all_gather(col_vecs, "row", axis=0, tiled=True),
        lax.all_gather(col_bias, "row", axis=0, tiled=True),
    )
    factor_width = row_full.shape[1]
    tile_edge = counts.shape[-1]
    slot_count = counts.shape[2]
    per_turn = 8
    row_tiles = row_full.reshape(-1, tile_edge, factor_width)
    row_shifts = row_shift_full.reshape(-1, tile_edge)
    col_tiles = col_full.reshape(-1, tile_edge, factor_width)
    col_shifts = col_shift_full.reshape(-1, tile_edge)
    row_ids = row_block.reshape(slot_count)
    col_ids = col_block.reshape(slot_count)
    count_tiles = counts.reshape(slot_count, tile_edge, tile_edge)
    col_here = lax.axis_index("col")
    row_here = lax.axis_index("row")
    own_total = block_totals[row_here, col_here]
    positions = jnp.arange(per_turn, dtype=jnp.int32)
    zero_partials = (
        jnp.zeros(row_tiles.shape, jnp.float32),
        jnp.zeros(col_tiles.shape, jnp.float32),
        jnp.zeros(row_shifts.shape, jnp.float32),
        jnp.zeros(col_shifts.shape, jnp.float32),
    )

    def local_turn(turn_index, partials):
        offset = turn_index * per_turn
        row_pick = lax.dynamic_slice_in_dim(row_ids, offset, per_turn, 0)
        col_pick = lax.dynamic_slice_in_dim(col_ids, offset, per_turn, 0)
        live_mask = (offset + positions < own_total).astype(jnp.float32)
        pieces = block_grads(
            lax.dynamic_slice_in_dim(count_tiles, offset, per_turn, 0),
            row_tiles[row_pick],
            col_tiles[col_pick],
            row_shifts[row_pick],
            col_shifts[col_pick],
            live_mask,
        )
        return accumulate(partials, row_pick, col_pick, pieces)

    turn_count = (own_total + per_turn - 1) // per_turn
    partials = lax.fori_loop(0, turn_count, local_turn, zero_partials)
    row_sum, row_bias_sum = (
        lax.psum_scatter(
            partials[0].reshape(-1, factor_width), "col", scatter_dimension=0, tiled=True
        ),
        lax.psum_scatter(partials[2].reshape(-1), "col", scatter_dimension=0, tiled=True),
    )
    col_sum, col_bias_sum = (
        lax.psum_scatter(
            partials[1].reshape(-1, factor_width), "row", scatter_dimension=0, tiled=True
        ),
        lax.psum_scatter(partials[3].reshape(-1), "row", scatter_dimension=0, tiled=True),
    )
    return (row_sum, row_bias_sum, col_sum, col_bias_sum)


def solution(mesh):
    placed = (
        P(("row", "col"), None),
        P(("row", "col")),
        P(("col", "row"), None),
        P(("col", "row")),
        P("row", "col", None),
        P("row", "col", None),
        P("row", "col", None, None, None),
        P(),
    )
    return jax.shard_map(
        body,
        mesh=mesh,
        in_specs=placed,
        out_specs=(
            P(("row", "col"), None),
            P(("row", "col")),
            P(("col", "row"), None),
            P(("col", "row")),
        ),
        check_vma=False,
    )
```

profile of v0, /device:TPU:1, one launch (start us, length us, event | category | flops | bytes accessed | tf_op | source)
XLA Modules:
  0.0 730.2 jit_solution(10085982067582367051)
XLA Ops:
  10.7 49.1 %all-gather.1 = bf16[32,1,128]{2,1,0:T(2,128)(2,1)S(1)} all-gather(bf16[1,1,128]{2,1,0:T(2,128)(2,1)} %bitcast.52), channel_id=1, replica_groups=mesh['col'=32,'row'=8] {'col'}, dimensions={0}, use_global_device_ids=true | all-gather | bytes 8448 | tf_op jit(solution)/shard_map/all_gather | solution.py:36
  63.3 27.7 %all-reduce = bf16[6400]{0:T(1024)(128)(2,1)} all-reduce(bf16[6400]{0:T(1024)(128)(2,1)S(1)} %dynamic-update-slice), channel_id=1, replica_groups=mesh['col'=32,'row'=8] {'row'}, use_global_device_ids=true, to_apply=%add | all-reduce | flops 6400 | bytes 25600
  91.0 4.6 copy.39
  95.6 32.9 %all-gather.7.cloned.1.call-done = bf16[8,800,300]{1,2,0:T(8,128)(2,1)} async-done(((bf16[1,800,300]{1,2,0:T(8,128)(2,1)}), bf16[8,800,300]{1,2,0:T(8,128)(2,1)}) %all-gather.7.cloned.1.call-update) | async-done | bytes 3840016 | tf_op jit(solution)/shard_map/all_gather | solution.py:39
  128.5 7.4 %copy.48 = bf16[8,800,300]{2,1,0:T(8,128)(2,1)} copy(bf16[8,800,300]{1,2,0:T(8,128)(2,1)} %all-gather.7.cloned.1.call-done) | data formatting | bytes 7680000
  142.6 356.6 %while.17 = (s32[]{:T(128)}, f32[32,128,300]{1,2,0:T(8,128)}, f32[50,128,300]{1,2,0:T(8,128)}, f32[32,128]{1,0:T(8,128)S(1)}, f32[50,128]{1,0:T(8,128)}, /*index...) while((s32[]{:T(128)}, f32[32,128,300]{1,2,0:T(8,128)}, ...), condition=%wide.region_7.8_spmd.clone, body=%wide.region_0.7_spmd.clone.sunk | while | flops 238252112 | bytes 16127003 | solution.py:80
  179.8 3.7 scatter_fusion
  202.1 3.7 scatter_fusion
  205.9 3.7 scatter_fusion.1
  224.5 3.7 scatter_fusion
  228.2 3.7 scatter_fusion.1
  317.2 3.8 scatter_fusion.1
  335.8 3.7 scatter_fusion
  402.5 3.7 scatter_fusion
  406.2 3.7 scatter_fusion.1
  428.5 3.7 scatter_fusion.1
  469.5 3.7 scatter_fusion
  491.8 3.7 scatter_fusion
  499.2 9.7 %copy.52 = f32[50,128,300]{2,1,0:T(8,128)} copy(f32[50,128,300]{1,2,0:T(8,128)} %get-tuple-element.87) | data formatting | bytes 15360000
  509.1 4.0 copy.58
  513.6 6.8 copy.55
  523.0 29.1 %all-reduce.2 = f32[6400]{0:T(1024)S(1)} all-reduce(f32[6400]{0:T(1024)} %bitcast.11), channel_id=5, replica_groups=mesh['col'=32,'row'=8] {'row'}, use_global_device_ids=true, to_apply=%region_11.12.clone | all-reduce | flops 6400 | bytes 51200
  552.8 142.4 %all-reduce.1 = f32[4096]{0:T(1024)S(1)} all-reduce(f32[4096]{0:T(1024)S(1)} %bitcast.50), channel_id=3, replica_groups=mesh['col'=32,'row'=8] {'col'}, use_global_device_ids=true, to_apply=%region_9.10.clone | all-reduce | flops 4096 | bytes 32768
  698.5 25.1 %reduce-scatter.5.cloned.1.call-done = f32[128,300]{0,1:T(8,128)} async-done(((f32[4096,300]{0,1:T(8,128)}), f32[128,300]{0,1:T(8,128)}) %reduce-scatter.5.cloned.1.call-update) | async-done | bytes 153616 | tf_op jit(solution)/shard_map/reduce_scatter | solution.py:82
  (350 shorter events, 329.3 us)
Async XLA Ops:
  7.2 83.8 %all-gather.5.cloned.1.call-start = ((), (), s32[]{:S(2)}) async-start(), calls=%async_computation.2 | async-start | bytes 2568192 | tf_op jit(solution)/shard_map/all_gather | solution.py:35
  7.9 120.6 %all-gather.7.cloned.1.call-start = ((), (), s32[]{:S(2)}) async-start(), calls=%async_computation.4 | async-start | bytes 4902912 | tf_op jit(solution)/shard_map/all_gather | solution.py:39
  8.6 687.2 %reduce-scatter.7.cloned.1.call-start = ((), (), s32[]{:S(2)}) async-start(), calls=%async_computation.5 | async-start | bytes 11059200
  144.0 12.7 %copy-start = (s32[8]{0:T(128)}, s32[8]{0:T(128)S(1)}, u32[]{:S(2)}) copy-start(s32[8]{0:T(128)S(1)} %get-tuple-element.264) | copy-start | bytes 100 | tf_op jit(solution)/shard_map/while
  144.0 12.7 %copy-start.1 = (s32[8]{0:T(128)}, s32[8]{0:T(128)S(1)}, u32[]{:S(2)}) copy-start(s32[8]{0:T(128)S(1)} %get-tuple-element.263) | copy-start | bytes 100 | tf_op jit(solution)/shard_map/while
  166.3 12.7 %copy-start.1 = (s32[8]{0:T(128)}, s32[8]{0:T(128)S(1)}, u32[]{:S(2)}) copy-start(s32[8]{0:T(128)S(1)} %get-tuple-element.263) | copy-start | bytes 100 | tf_op jit(solution)/shard_map/while
  188.6 12.7 %copy-start = (s32[8]{0:T(128)}, s32[8]{0:T(128)S(1)}, u32[]{:S(2)}) copy-start(s32[8]{0:T(128)S(1)} %get-tuple-element.264) | copy-start | bytes 100 | tf_op jit(solution)/shard_map/while
  188.6 12.7 %copy-start.1 = (s32[8]{0:T(128)}, s32[8]{0:T(128)S(1)}, u32[]{:S(2)}) copy-start(s32[8]{0:T(128)S(1)} %get-tuple-element.263) | copy-start | bytes 100 | tf_op jit(solution)/shard_map/while
  211.0 12.7 %copy-start.1 = (s32[8]{0:T(128)}, s32[8]{0:T(128)S(1)}, u32[]{:S(2)}) copy-start(s32[8]{0:T(128)S(1)} %get-tuple-element.263) | copy-start | bytes 100 | tf_op jit(solution)/shard_map/while
  233.3 12.7 %copy-start = (s32[8]{0:T(128)}, s32[8]{0:T(128)S(1)}, u32[]{:S(2)}) copy-start(s32[8]{0:T(128)S(1)} %get-tuple-element.264) | copy-start | bytes 100 | tf_op jit(solution)/shard_map/while
  233.3 12.7 %copy-start.1 = (s32[8]{0:T(128)}, s32[8]{0:T(128)S(1)}, u32[]{:S(2)}) copy-start(s32[8]{0:T(128)S(1)} %get-tuple-element.263) | copy-start | bytes 100 | tf_op jit(solution)/shard_map/while
  255.4 12.7 %copy-start = (s32[8]{0:T(128)}, s32[8]{0:T(128)S(1)}, u32[]{:S(2)}) copy-start(s32[8]{0:T(128)S(1)} %get-tuple-element.264) | copy-start | bytes 100 | tf_op jit(solution)/shard_map/while
  255.4 12.7 %copy-start.1 = (s32[8]{0:T(128)}, s32[8]{0:T(128)S(1)}, u32[]{:S(2)}) copy-start(s32[8]{0:T(128)S(1)} %get-tuple-element.263) | copy-start | bytes 100 | tf_op jit(solution)/shard_map/while
  277.7 12.7 %copy-start = (s32[8]{0:T(128)}, s32[8]{0:T(128)S(1)}, u32[]{:S(2)}) copy-start(s32[8]{0:T(128)S(1)} %get-tuple-element.264) | copy-start | bytes 100 | tf_op jit(solution)/shard_map/while
  277.7 12.7 %copy-start.1 = (s32[8]{0:T(128)}, s32[8]{0:T(128)S(1)}, u32[]{:S(2)}) copy-start(s32[8]{0:T(128)S(1)} %get-tuple-element.263) | copy-start | bytes 100 | tf_op jit(solution)/shard_map/while
  300.0 12.7 %copy-start = (s32[8]{0:T(128)}, s32[8]{0:T(128)S(1)}, u32[]{:S(2)}) copy-start(s32[8]{0:T(128)S(1)} %get-tuple-element.264) | copy-start | bytes 100 | tf_op jit(solution)/shard_map/while
  300.0 12.7 %copy-start.1 = (s32[8]{0:T(128)}, s32[8]{0:T(128)S(1)}, u32[]{:S(2)}) copy-start(s32[8]{0:T(128)S(1)} %get-tuple-element.263) | copy-start | bytes 100 | tf_op jit(solution)/shard_map/while
  322.3 12.7 %copy-start.1 = (s32[8]{0:T(128)}, s32[8]{0:T(128)S(1)}, u32[]{:S(2)}) copy-start(s32[8]{0:T(128)S(1)} %get-tuple-element.263) | copy-start | bytes 100 | tf_op jit(solution)/shard_map/while
  344.6 12.7 %copy-start.1 = (s32[8]{0:T(128)}, s32[8]{0:T(128)S(1)}, u32[]{:S(2)}) copy-start(s32[8]{0:T(128)S(1)} %get-tuple-element.263) | copy-start | bytes 100 | tf_op jit(solution)/shard_map/while
  411.3 12.7 %copy-start.1 = (s32[8]{0:T(128)}, s32[8]{0:T(128)S(1)}, u32[]{:S(2)}) copy-start(s32[8]{0:T(128)S(1)} %get-tuple-element.263) | copy-start | bytes 100 | tf_op jit(solution)/shard_map/while
  433.7 12.7 %copy-start.1 = (s32[8]{0:T(128)}, s32[8]{0:T(128)S(1)}, u32[]{:S(2)}) copy-start(s32[8]{0:T(128)S(1)} %get-tuple-element.263) | copy-start | bytes 100 | tf_op jit(solution)/shard_map/while
  456.0 12.7 %copy-start.1 = (s32[8]{0:T(128)}, s32[8]{0:T(128)S(1)}, u32[]{:S(2)}) copy-start(s32[8]{0:T(128)S(1)} %get-tuple-element.263) | copy-start | bytes 100 | tf_op jit(solution)/shard_map/while
  478.3 12.7 %copy-start.1 = (s32[8]{0:T(128)}, s32[8]{0:T(128)S(1)}, u32[]{:S(2)}) copy-start(s32[8]{0:T(128)S(1)} %get-tuple-element.263) | copy-start | bytes 100 | tf_op jit(solution)/shard_map/while
  508.9 214.8 %reduce-scatter.5.cloned.1.call-start = ((), (), s32[]{:S(2)}) async-start(), calls=%async_computation.3 | async-start | bytes 5136384 | tf_op jit(solution)/shard_map/reduce_scatter | solution.py:82
  (13 other events, 153.1 us)
Sparse Core Ops, SparseCore 0:
  10.5 61.5 all-gather.4
  73.8 54.6 all-gather.6
  509.0 108.3 reduce-scatter.6
  622.5 101.1 reduce-scatter.4
where the time goes:
time: 737 us; the launch traced here: 730 us
  blocking collectives  248 us (34%)
  other arithmetic  182 us (25%)
  local copies, waits for them, and re-layouts  181 us (25%)
  waiting for transfers between devices  59.5 us (8%)
  matrix products  41.3 us (6%)
  between operations  16.5 us (2%)
    unnamed x3, blocking collectives  199 us
    scatter-add x16, other arithmetic, accumulate(): partials[1].at[col_pick].add(pieces[1])  59 us
    scatter-add x16, other arithmetic, accumulate(): partials[0].at[row_pick].add(pieces[0])  58.9 us
    gather x16, local copies, waits for them, and re-layouts, local_turn(): col_tiles[col_pick]  49.8 us
    all_gather x1, blocking collectives, body(): lax.all_gather(row_bias, 'col', axis=0, tiled=True)  49.1 us
    gather x16, local copies, waits for them, and re-layouts, local_turn(): row_tiles[row_pick]  41.7 us
    all_gather x1, waiting for transfers between devices, body(): lax.all_gather(col_vecs, 'row', axis=0, tiled=True)  32.9 us
    unnamed x14, local copies, waits for them, and re-layouts  32.4 us
  transfers between devices with their start and end apart: 4, of which 2 were waited for; matrix products, arithmetic and copies ran while one was open for 3% of the time, Pallas kernels for 0%

commit v1 on v0

v1 whole, which is shorter than its diff:
```python
import functools

import jax
import jax.numpy as jnp
from jax import lax
from jax.experimental import pallas as pl
from jax.experimental.pallas import tpu as pltpu
from jax.sharding import PartitionSpec as P

MESH = pl.DeviceIdType.MESH
ANY = pl.BlockSpec(memory_space=pl.ANY)
IN_VMEM = pl.BlockSpec(memory_space=pltpu.VMEM)
F32, BF16 = jnp.float32, jnp.bfloat16

D = 300
DP = 304
L = 128
SHARD = 800
FULL = SHARD // L
QR = 80
PACK = FULL * DP + QR
HALF = 960
RHALF = 160
SHARDS = 8
ROW_TILES = 32
COL_TILES = 50
CAP = 128
GROUP = 8
VMEM_LIMIT = 56 * 1024 * 1024


def place():
    row, col = lax.axis_index("row"), lax.axis_index("col")
    y, zl = row % 4, row // 4
    core, x, zh = col % 2, (col // 2) % 4, col // 8
    return y, zl, core, x, zh


def row_of(y, zl):
    return zl * 4 + y


def col_of(core, x, zh):
    return (zh * 4 + x) * 2 + core


class Ring:
    def __init__(self, send, recv):
        self.send, self.recv = send, recv
        self.y, self.zl, self.core, self.x, self.zh = place()
        y, zl, core, x, zh = self.y, self.zl, self.core, self.x, self.zh
        row, col = row_of(y, zl), col_of(core, x, zh)
        self.near = {
            "y+": (row_of((y + 1) % 4, zl), col),
            "y-": (row_of((y + 3) % 4, zl), col),
            "zl": (row_of(y, 1 - zl), col),
            "x+": (row, col_of(core, (x + 1) % 4, zh)),
            "x-": (row, col_of(core, (x + 3) % 4, zh)),
            "zh+": (row, col_of(core, x, (zh + 1) % 4)),
            "zh-": (row, col_of(core, x, (zh + 3) % 4)),
            "core": (row, col_of(1 - core, x, zh)),
        }
        self.started = []

    def greet(self):
        barrier = pltpu.get_barrier_semaphore()
        for row, col in self.near.values():
            pl.semaphore_signal(barrier, inc=1, device_id={"row": row, "col": col}, device_id_type=MESH)
        return barrier

    def meet(self, barrier):
        pl.semaphore_wait(barrier, len(self.near))

    def copy(self, k, to, src, dst):
        row, col = self.near[to]
        out = pltpu.make_async_remote_copy(
            src_ref=src,
            dst_ref=dst,
            send_sem=self.send.at[k],
            recv_sem=self.recv.at[k],
            device_id={"row": row, "col": col},
            device_id_type=MESH,
        )
        out.start()
        self.started.append(out)
        return out

    def finish(self):
        for out in self.started:
            out.wait_send()


def gather_kernel(ct_ref, rt_ref, gc_ref, gr_ref, wc, send, recv, local):
    ring = Ring(send, recv)
    y, zl, core, x, zh = ring.y, ring.zl, ring.core, ring.x, ring.zh
    barrier = ring.greet()
    for t in range(FULL):
        wc[t * DP : (t + 1) * DP] = ct_ref[0:DP, t * L : (t + 1) * L]
    tail = ct_ref[0:QR, FULL * L : (FULL + 1) * L].astype(F32)
    for q in range(1, 4):
        part = ct_ref[q * QR : (q + 1) * QR, FULL * L : (FULL + 1) * L].astype(F32)
        tail = tail + pltpu.roll(part, 32 * q, 1)
    wc[FULL * DP : PACK] = tail.astype(BF16)
    mine = row_of(y, zl)
    other = row_of(y, 1 - zl)
    up, down, far = (y + 1) % 4, (y + 3) % 4, (y + 2) % 4
    own_c = pltpu.make_async_copy(wc, gc_ref.at[mine], local.at[0])
    own_r = pltpu.make_async_copy(rt_ref, gr_ref.at[core, x, zh], local.at[1])
    own_c.start()
    own_r.start()
    ring.meet(barrier)
    c_y0 = ring.copy(0, "y+", wc, gc_ref.at[mine])
    c_y1 = ring.copy(1, "y-", wc, gc_ref.at[mine])
    r_z0 = ring.copy(2, "zh+", rt_ref, gr_ref.at[core, x, zh])
    r_z1 = ring.copy(3, "zh-", rt_ref, gr_ref.at[core, x, zh])
    c_z = ring.copy(4, "zl", wc, gc_ref.at[mine])

    lo, hi = pl.ds(0, RHALF), pl.ds(RHALF, DP - RHALF)
    r_z0.wait_recv()
    part = gr_ref.at[core, x, (zh + 3) % 4, lo]
    r_z2 = ring.copy(5, "zh+", part, part)
    r_z1.wait_recv()
    part = gr_ref.at[core, x, (zh + 1) % 4, hi]
    r_z3 = ring.copy(6, "zh-", part, part)
    r_z2.wait_recv()
    r_z3.wait_recv()
    own_r.wait()
    part = gr_ref.at[core, x]
    r_x0 = ring.copy(7, "x+", part, part)
    r_x1 = ring.copy(8, "x-", part, part)
    r_c0 = ring.copy(9, "core", part, part)

    lo, hi = pl.ds(0, HALF), pl.ds(HALF, PACK - HALF)
    c_y0.wait_recv()
    part = gc_ref.at[row_of(down, zl), lo]
    c_y2 = ring.copy(10, "y+", part, part)
    c_y1.wait_recv()
    part = gc_ref.at[row_of(up, zl), hi]
    c_y3 = ring.copy(11, "y-", part, part)
    c_z.wait_recv()
    part = gc_ref.at[other]
    c_y4 = ring.copy(12, "y+", part, part)
    c_y5 = ring.copy(13, "y-", part, part)

    r_x0.wait_recv()
    part = gr_ref.at[core, (x + 3) % 4, pl.ds(0, 2)]
    r_x2 = ring.copy(14, "x+", part, part)
    part = gr_ref.at[core, (x + 3) % 4]
    r_c1 = ring.copy(15, "core", part, part)
    r_x1.wait_recv()
    part = gr_ref.at[core, (x + 1) % 4, pl.ds(2, 2)]
    r_x3 = ring.copy(16, "x-", part, part)
    part = gr_ref.at[core, (x + 1) % 4]
    r_c2 = ring.copy(17, "core", part, part)
    r_x2.wait_recv()
    r_x3.wait_recv()
    part = gr_ref.at[core, (x + 2) % 4]
    r_c3 = ring.copy(18, "core", part, part)

    c_y2.wait_recv()
    c_y3.wait_recv()
    part = gc_ref.at[row_of(far, zl)]
    c_z1 = ring.copy(19, "zl", part, part)

    for done in (r_c0, r_c1, r_c2, r_c3, c_y4, c_y5, c_z1):
        done.wait_recv()
    ring.finish()
    own_c.wait()


def gather(ct, rt):
    return pl.pallas_call(
        gather_kernel,
        out_shape=(
            jax.ShapeDtypeStruct((SHARDS, PACK, L), BF16),
            jax.ShapeDtypeStruct((2, 4, 4, DP, L), BF16),
        ),
        in_specs=[IN_VMEM, IN_VMEM],
        out_specs=(ANY, ANY),
        scratch_shapes=[
            pltpu.VMEM((PACK, L), BF16),
            pltpu.SemaphoreType.DMA((20,)),
            pltpu.SemaphoreType.DMA((20,)),
            pltpu.SemaphoreType.DMA((2,)),
        ],
        compiler_params=pltpu.CompilerParams(
            collective_id=0, has_side_effects=True, vmem_limit_bytes=VMEM_LIMIT
        ),
        name="gather",
    )(ct, rt)


def shards_to_tiles(packed, tiles):
    lane = lax.broadcasted_iota(jnp.int32, (DP, L), 1)
    at, carry = 0, None
    for s in range(SHARDS):
        shift = (32 * s) % L
        for t in range(FULL):
            cur = packed[s, t * DP : (t + 1) * DP].astype(F32)
            if shift:
                cur = pltpu.roll(cur, shift, 1)
                tiles[at] = jnp.where(lane < shift, carry, cur).astype(BF16)
            else:
                tiles[at] = cur.astype(BF16)
            at, carry = at + 1, cur
        tail = packed[s, FULL * DP : PACK].astype(F32)
        parts = [pltpu.roll(tail, (shift - 32 * q) % L, 1) if (shift - 32 * q) % L else tail for q in range(4)]
        cur = jnp.concatenate(parts, axis=0)[:DP]
        if shift:
            cur = jnp.where(lane < shift, carry, cur)
        if shift + 32 == L:
            tiles[at] = cur.astype(BF16)
            at, carry = at + 1, None
        else:
            carry = cur


def tiles_to_shards(tiles, packed):
    lane = lax.broadcasted_iota(jnp.int32, (DP, L), 1)
    lane_q = lax.broadcasted_iota(jnp.int32, (QR, L), 1)
    for s in range(SHARDS):
        shift = (32 * s) % L
        base = (SHARD * s) // L
        cur = tiles[base]
        if shift:
            cur = pltpu.roll(cur, L - shift, 1)
        for t in range(FULL):
            nxt = tiles[base + t + 1]
            if shift:
                nxt = pltpu.roll(nxt, L - shift, 1)
                packed[s, t * DP : (t + 1) * DP] = jnp.where(lane < L - shift, cur, nxt).astype(BF16)
            else:
                packed[s, t * DP : (t + 1) * DP] = cur.astype(BF16)
            cur = nxt
        cur = jnp.concatenate([cur, jnp.zeros((4 * QR - DP, L), F32)], axis=0)
        tail = cur[:QR]
        for q in range(1, 4):
            tail = jnp.where(lane_q < 32 * q, tail, pltpu.roll(cur[q * QR : (q + 1) * QR], 32 * q, 1))
        packed[s, FULL * DP : PACK] = tail.astype(BF16)


LOG2_100 = 6.643856189774724
LN2 = 0.6931471805599453


def blocks_kernel(total_ref, rid_ref, cid_ref, counts_ref, gc_ref, gr_ref, pc_ref, pr_ref,
                  counts, packed, rt, rn, ct, acc_c, acc_r, sems, count_sems):
    row, col = lax.axis_index("row"), lax.axis_index("col")
    total = total_ref[row, col]
    groups = (total + GROUP - 1) // GROUP
    load_r = pltpu.make_async_copy(gr_ref, rt, sems.at[0])
    load_c = pltpu.make_async_copy(gc_ref, packed, sems.at[1])
    load_r.start()
    load_c.start()

    def load(g):
        part = pl.ds(g * GROUP, GROUP)
        return pltpu.make_async_copy(counts_ref.at[part], counts.at[part], count_sems.at[g])

    @pl.loop(0, groups)
    def _(g):
        load(g).start()

    @pl.loop(0, COL_TILES)
    def _(i):
        acc_c[i] = jnp.zeros((DP, L), F32)

    @pl.loop(0, ROW_TILES)
    def _(i):
        acc_r[i] = jnp.zeros((DP, L), F32)

    load_r.wait()

    @pl.loop(0, ROW_TILES)
    def _(i):
        rn[i] = rt[i].astype(F32).T.astype(BF16)

    load_c.wait()
    shards_to_tiles(packed, ct)

    @pl.loop(0, groups)
    def _(g):
        load(g).wait()
        terms, rids, cids = [], [], []
        for k in range(GROUP):
            n = g * GROUP + k
            rid, cid = rid_ref[n], cid_ref[n]
            rids.append(rid)
            cids.append(cid)
            scores = jnp.dot(rn[rid], ct[cid], preferred_element_type=F32)
            x = counts[n]
            least = jnp.where(n < total, 0, jnp.int32(2**31 - 1))
            log2x = jnp.log2(jnp.maximum(x.astype(F32), 1.0))
            weight2 = jnp.exp2(jnp.minimum(0.75 * log2x + (1.0 - 0.75 * LOG2_100), 1.0))
            term = weight2 * (scores - LN2 * log2x)
            terms.append(jnp.where(x > least, term, 0.0).astype(BF16))
        for k in range(GROUP):
            acc_c[cids[k]] += jnp.dot(rt[rids[k]], terms[k], preferred_element_type=F32)
            acc_r[rids[k]] += lax.dot_general(
                ct[cids[k]], terms[k], (((1,), (1,)), ((), ())), preferred_element_type=F32
            )

    tiles_to_shards(acc_c, packed)
    out_c = pltpu.make_async_copy(packed, pc_ref, sems.at[0])
    out_r = pltpu.make_async_copy(acc_r, pr_ref, sems.at[1])
    out_c.start()
    out_r.start()
    out_c.wait()
    out_r.wait()


def blocks(totals, rid, cid, counts, gc, gr):
    smem = pl.BlockSpec(memory_space=pltpu.SMEM)
    return pl.pallas_call(
        blocks_kernel,
        out_shape=(
            jax.ShapeDtypeStruct((SHARDS, PACK, L), BF16),
            jax.ShapeDtypeStruct((ROW_TILES, DP, L), F32),
        ),
        in_specs=[smem, smem, smem, ANY, ANY, ANY],
        out_specs=(ANY, ANY),
        scratch_shapes=[
            pltpu.VMEM((CAP, L, L), jnp.int32),
            pltpu.VMEM((SHARDS, PACK, L), BF16),
            pltpu.VMEM((ROW_TILES, DP, L), BF16),
            pltpu.VMEM((ROW_TILES, L, DP), BF16),
            pltpu.VMEM((COL_TILES, DP, L), BF16),
            pltpu.VMEM((COL_TILES, DP, L), F32),
            pltpu.VMEM((ROW_TILES, DP, L), F32),
            pltpu.SemaphoreType.DMA((2,)),
            pltpu.SemaphoreType.DMA((CAP // GROUP,)),
        ],
        compiler_params=pltpu.CompilerParams(vmem_limit_bytes=VMEM_LIMIT),
        name="blocks",
    )(totals, rid, cid, counts, gc, gr)


def reduce_kernel(pc_ref, pr_ref, oc_ref, obc_ref, or_ref, obr_ref,
                  pc, pr, got_c, half_c, put_c, got_core, got_x, put_x, half_x, half_z, got_z, put_z, u,
                  send, recv, local):
    ring = Ring(send, recv)
    y, zl, core, x, zh = ring.y, ring.zl, ring.core, ring.x, ring.zh
    zo = 1 - zl
    barrier = ring.greet()
    up, down, far = (y + 1) % 4, (y + 3) % 4, (y + 2) % 4
    xu, xd, xf = (x + 1) % 4, (x + 3) % 4, (x + 2) % 4
    zu, zd, zf = (zh + 1) % 4, (zh + 3) % 4, (zh + 2) % 4
    wanted = (row_of(far, zl), row_of(up, zl), row_of(down, zl), row_of(y, zo), row_of(y, zl))
    loads = [pltpu.make_async_copy(pc_ref.at[w], pc.at[i], local.at[i]) for i, w in enumerate(wanted)]
    load_r = pltpu.make_async_copy(pr_ref.at[core], pr, local.at[5])
    loads[0].start()
    load_r.start()
    for k in range(1, 5):
        loads[k].start()
    ring.meet(barrier)
    a_z = ring.copy(0, "zl", pc_ref.at[row_of(far, zo)], got_c.at[0])
    a_y0 = ring.copy(1, "y+", pc_ref.at[row_of(up, zo)], got_c.at[1])
    a_y1 = ring.copy(2, "y-", pc_ref.at[row_of(down, zo)], got_c.at[2])
    b_c = [
        ring.copy(3 + k, "core", pr_ref.at[1 - core, w], got_core.at[k])
        for k, w in enumerate((xf, xu, xd, x))
    ]
    load_r.wait()

    b_c[0].wait_recv()
    for z in range(4):
        put_x[0, z] = (pr[xf, z] + got_core[0, z]).astype(BF16)
    b_x0 = ring.copy(7, "x+", put_x.at[0, pl.ds(0, 2)], half_x.at[0])
    b_x1 = ring.copy(8, "x-", put_x.at[0, pl.ds(2, 2)], half_x.at[1])

    b_c[1].wait_recv()
    b_x0.wait_recv()
    for z in range(4):
        total = pr[xu, z] + got_core[1, z]
        if z < 2:
            total = total + half_x[0, z].astype(F32)
        put_x[1, z] = total.astype(BF16)
    b_x2 = ring.copy(9, "x+", put_x.at[1], got_x.at[0])
    b_c[2].wait_recv()
    b_x1.wait_recv()
    for z in range(4):
        total = pr[xd, z] + got_core[2, z]
        if z >= 2:
            total = total + half_x[1, z - 2].astype(F32)
        put_x[2, z] = total.astype(BF16)
    b_x3 = ring.copy(10, "x-", put_x.at[2], got_x.at[1])

    loads[0].wait()
    a_z.wait_recv()
    put_c[0] = (pc[0].astype(F32) + got_c[0].astype(F32)).astype(BF16)
    lo, hi = pl.ds(0, HALF), pl.ds(HALF, PACK - HALF)
    a_y2 = ring.copy(11, "y+", put_c.at[0, lo], half_c.at[lo])
    a_y3 = ring.copy(12, "y-", put_c.at[0, hi], half_c.at[hi])

    loads[3].wait()
    a_y0.wait_recv()
    a_y1.wait_recv()
    put_c[1] = (pc[3].astype(F32) + got_c[1].astype(F32) + got_c[2].astype(F32)).astype(BF16)
    a_z1 = ring.copy(13, "zl", put_c.at[1], got_c.at[3])

    b_c[3].wait_recv()
    b_x2.wait_recv()
    b_x3.wait_recv()
    for z in range(4):
        u[z] = pr[x, z] + got_core[3, z] + got_x[0, z].astype(F32) + got_x[1, z].astype(F32)
    put_z[0] = u[zf].astype(BF16)
    rlo, rhi = pl.ds(0, RHALF), pl.ds(RHALF, DP - RHALF)
    b_z0 = ring.copy(14, "zh+", put_z.at[0, rlo], half_z.at[rlo])
    b_z1 = ring.copy(15, "zh-", put_z.at[0, rhi], half_z.at[rhi])

    loads[1].wait()
    a_y2.wait_recv()
    put_c[2, 0:HALF] = (pc[1, 0:HALF].astype(F32) + half_c[0:HALF].astype(F32)).astype(BF16)
    put_c[2, HALF:PACK] = pc[1, HALF:PACK]
    a_y4 = ring.copy(16, "y+", put_c.at[2], got_c.at[4])
    loads[2].wait()
    a_y3.wait_recv()
    put_c[3, 0:HALF] = pc[2, 0:HALF]
    put_c[3, HALF:PACK] = (pc[2, HALF:PACK].astype(F32) + half_c[HALF:PACK].astype(F32)).astype(BF16)
    a_y5 = ring.copy(17, "y-", put_c.at[3], got_c.at[5])

    b_z0.wait_recv()
    put_z[1, 0:RHALF] = (u[zu, 0:RHALF] + half_z[0:RHALF].astype(F32)).astype(BF16)
    put_z[1, RHALF:DP] = u[zu, RHALF:DP].astype(BF16)
    b_z2 = ring.copy(18, "zh+", put_z.at[1], got_z.at[0])
    b_z1.wait_recv()
    put_z[2, 0:RHALF] = u[zd, 0:RHALF].astype(BF16)
    put_z[2, RHALF:DP] = (u[zd, RHALF:DP] + half_z[RHALF:DP].astype(F32)).astype(BF16)
    b_z3 = ring.copy(19, "zh-", put_z.at[2], got_z.at[1])

    b_z2.wait_recv()
    b_z3.wait_recv()
    row_sum = u[zh] + got_z[0].astype(F32) + got_z[1].astype(F32)
    or_ref[...] = row_sum[:D]
    obr_ref[...] = row_sum[D : D + 1]

    loads[4].wait()
    a_z1.wait_recv()
    a_y4.wait_recv()
    a_y5.wait_recv()

    def col_sum(start, size):
        part = slice(start, start + size)
        return (
            pc[4, part].astype(F32) + got_c[3, part].astype(F32)
            + got_c[4, part].astype(F32) + got_c[5, part].astype(F32)
        )

    for t in range(FULL):
        total = col_sum(t * DP, DP)
        oc_ref[:, t * L : (t + 1) * L] = total[:D]
        obc_ref[:, t * L : (t + 1) * L] = total[D + 1 : D + 2]
    tail = col_sum(FULL * DP, QR)
    for q in range(4):
        part = pltpu.roll(tail, L - 32 * q, 1) if q else tail
        rows = min(QR, D - q * QR)
        oc_ref[q * QR : q * QR + rows, FULL * L : SHARD] = part[:rows, : SHARD - FULL * L]
        if q == 3:
            obc_ref[:, FULL * L : SHARD] = part[rows + 1 : rows + 2, : SHARD - FULL * L]
    ring.finish()


def reduce(pc, pr):
    return pl.pallas_call(
        reduce_kernel,
        out_shape=(
            jax.ShapeDtypeStruct((D, SHARD), F32),
            jax.ShapeDtypeStruct((1, SHARD), F32),
            jax.ShapeDtypeStruct((D, L), F32),
            jax.ShapeDtypeStruct((1, L), F32),
        ),
        in_specs=[ANY, ANY],
        out_specs=(IN_VMEM,) * 4,
        scratch_shapes=[
            pltpu.VMEM((5, PACK, L), BF16),
            pltpu.VMEM((4, 4, DP, L), F32),
            pltpu.VMEM((6, PACK, L), BF16),
            pltpu.VMEM((PACK, L), BF16),
            pltpu.VMEM((4, PACK, L), BF16),
            pltpu.VMEM((4, 4, DP, L), F32),
            pltpu.VMEM((2, 4, DP, L), BF16),
            pltpu.VMEM((3, 4, DP, L), BF16),
            pltpu.VMEM((2, 2, DP, L), BF16),
            pltpu.VMEM((DP, L), BF16),
            pltpu.VMEM((2, DP, L), BF16),
            pltpu.VMEM((3, DP, L), BF16),
            pltpu.VMEM((4, DP, L), F32),
            pltpu.SemaphoreType.DMA((20,)),
            pltpu.SemaphoreType.DMA((20,)),
            pltpu.SemaphoreType.DMA((6,)),
        ],
        compiler_params=pltpu.CompilerParams(
            collective_id=1, has_side_effects=True, vmem_limit_bytes=VMEM_LIMIT
        ),
        name="reduce",
    )(pc, pr)


def pad_to(a, rows, lanes):
    return jnp.pad(a, ((0, rows - a.shape[0]), (0, lanes - a.shape[1])))


def body(row_vecs, row_bias, col_vecs, col_bias, row_block, col_block, counts, block_totals):
    one_c, one_r = jnp.ones((1, SHARD), BF16), jnp.ones((1, L), BF16)
    ct = pad_to(jnp.concatenate([col_vecs.T, one_c, col_bias[None]], axis=0), 4 * QR, (FULL + 1) * L)
    rt = pad_to(jnp.concatenate([row_vecs.T, row_bias[None], one_r], axis=0), DP, L)
    gc, gr = gather(ct, rt)
    rid = row_block.reshape(CAP)
    rid = (rid % 2) * 16 + (rid // 2) % 4 * 4 + rid // 8
    cid = col_block.reshape(CAP)
    pc, pr = blocks(block_totals, rid, cid, counts.reshape(CAP, L, L), gc, gr.reshape(ROW_TILES, DP, L))
    oc, obc, orow, obr = reduce(pc, pr.reshape(2, 4, 4, DP, L))
    return orow.T, obr.reshape(L), oc.T, obc.reshape(SHARD)


def solution(mesh):
    placed = (
        P(("row", "col"), None),
        P(("row", "col")),
        P(("col", "row"), None),
        P(("col", "row")),
        P("row", "col", None),
        P("row", "col", None),
        P("row", "col", None, None, None),
        P(),
    )
    return jax.shard_map(
        body,
        mesh=mesh,
        in_specs=placed,
        out_specs=(
            P(("row", "col"), None),
            P(("row", "col")),
            P(("col", "row"), None),
            P(("col", "row")),
        ),
        check_vma=False,
    )
```

time: 737 us -> 129 us (0.18)
  the two profiles are of different devices: /device:TPU:1 before, /device:TPU:66 now
where the time goes in v1:
time: 129 us; the launch traced here: 128 us
  Pallas kernels  116 us (90%)
  local copies, waits for them, and re-layouts  7.39 us (6%)
  other arithmetic  4.68 us (4%)
    pallas_call x1, Pallas kernels, gather(): pl.pallas_call(gather_kernel, out_shape=(jax.ShapeDtypeStruct((SHARDS, PA...  49.3 us
    pallas_call x1, Pallas kernels, reduce(): pl.pallas_call(reduce_kernel, out_shape=(jax.ShapeDtypeStruct((D, SHARD),...  45 us
    pallas_call x1, Pallas kernels, blocks(): pl.pallas_call(blocks_kernel, out_shape=(jax.ShapeDtypeStruct((SHARDS, PA...  21.2 us
    unnamed x3, local copies, waits for them, and re-layouts  5.05 us

profile of v1, /device:TPU:66, one launch (start us, length us, event | category | flops | bytes accessed | tf_op | source)
XLA Modules:
  0.0 128.3 jit_solution(6684901866069990834)
XLA Ops:
  0.6 1.2 fusion.2.rid_ref
  1.8 0.1 pad.12.clone
  1.9 0.1 pad.14.clone
  2.0 0.7 broadcast_in_dim.13
  2.7 1.0 maximum_maximum_fusion
  3.7 0.6 pad.9.rt_ref
  4.3 1.2 pad_maximum_fusion
  5.5 0.9 pad.8.ct_ref
  6.4 49.3 %gather.1 = (bf16[8,1904,128]{2,1,0:T(8,128)(2,1)}, bf16[2,4,4,304,128]{4,3,2,1,0:T(8,128)(2,1)}) custom-call(bf16[320,896]{1,0:T(8,128)(2,1)} %pad.8.ct_ref, bf16[304,128]{1,0:T(8,128)(2,1)} %pad.9.rt_ref), custom_call_target="tpu_custom_call" | custom-call | tf_op jit(solution)/shard_map/gather/pallas_call | solution.py:172
  55.7 21.2 %blocks.1 = (bf16[8,1904,128]{2,1,0:T(8,128)(2,1)}, f32[32,304,128]{2,1,0:T(8,128)}) custom-call(s32[8,32]{1,0:T(8,128)} %total_ref.1, s32[128]{0:T(128)} %fusion.2.rid_ref, s32[128]{0:T(128)} %bitcast.36, s32[128,128,128]{2,1,0:T(8,128)} %bitcast.28, bf16[8,1904,128]{2,1,0:T(8,128)(2,1)} %get-tuple-element.12.gc_ref, bf16[32,304,128]{2,1,0:T(8,128)(2,1)} %bitcast.30), custom_call_target="tpu_custom_call" | custom-call | tf_op jit(solution)/shard_map/blocks/pallas_call | solution.py:314
  77.0 45.0 %reduce.2 = (f32[300,800]{1,0:T(8,128)}, f32[1,800]{1,0:T(1,128)}, f32[300,128]{1,0:T(8,128)}, f32[1,128]{1,0:T(1,128)}) custom-call(bf16[8,1904,128]{2,1,0:T(8,128)(2,1)} %get-tuple-element.14.pc_ref, f32[2,4,4,304,128]{4,3,2,1,0:T(8,128)} %bitcast.29), custom_call_target="tpu_custom_call" | custom-call | tf_op jit(solution)/shard_map/reduce/pallas_call | solution.py:464
  121.9 1.3 %reduce.1 = f32[800]{0:T(1024)} reduce(f32[1,800]{1,0:T(1,128)} %get-tuple-element.19, f32[]{:T(128)} %constant.67), dimensions={0}, to_apply=%get-tuple-element.19.reduce_sub_computation | reduce | bytes 6404 | tf_op jit(solution)/shard_map/reduce/pallas_call | solution.py:464
  123.2 1.6 %copy.15 = f32[128,300]{0,1:T(8,128)} copy(f32[128,300]{0,1:T(8,128)} %bitcast.33) | data formatting | bytes 307200
  124.8 1.2 copy.16
  126.0 2.3 %copy.17 = f32[800,300]{0,1:T(8,128)} copy(f32[800,300]{0,1:T(8,128)} %bitcast.31) | data formatting | bytes 1920000

commit v2 on v1

v2 whole, which is shorter than its diff:
```python
import jax
import jax.numpy as jnp
from jax import lax
from jax.experimental import pallas as pl
from jax.experimental.pallas import tpu as pltpu
from jax.sharding import PartitionSpec as P

MESH = pl.DeviceIdType.MESH
ANY = pl.BlockSpec(memory_space=pl.ANY)
IN_VMEM = pl.BlockSpec(memory_space=pltpu.VMEM)
IN_SMEM = pl.BlockSpec(memory_space=pltpu.SMEM)
F32, BF16 = jnp.float32, jnp.bfloat16

D = 300
DP = 304
L = 128
SHARD = 800
FULL = SHARD // L
REST = SHARD - FULL * L
QR = 80
PACK = FULL * DP + QR
CUTS = (0, 480, 960, 1440, PACK)
RHALF = 160
SHARDS = 8
ROW_TILES = 32
COL_TILES = 50
QUAD = COL_TILES // 2
CAP = 128
GROUP = 8
VMEM_LIMIT = 56 * 1024 * 1024


def chunk(c):
    return pl.ds(CUTS[c], CUTS[c + 1] - CUTS[c])


def place():
    row, col = lax.axis_index("row"), lax.axis_index("col")
    y, zl = row % 4, row // 4
    core, x, zh = col % 2, (col // 2) % 4, col // 8
    return y, zl, core, x, zh


def row_of(y, zl):
    return zl * 4 + y


def col_of(core, x, zh):
    return (zh * 4 + x) * 2 + core


class Ring:
    def __init__(self, send, recv):
        self.send, self.recv = send, recv
        self.y, self.zl, self.core, self.x, self.zh = place()
        y, zl, core, x, zh = self.y, self.zl, self.core, self.x, self.zh
        row, col = row_of(y, zl), col_of(core, x, zh)
        self.near = {
            "y+": (row_of((y + 1) % 4, zl), col),
            "y-": (row_of((y + 3) % 4, zl), col),
            "zl": (row_of(y, 1 - zl), col),
            "x+": (row, col_of(core, (x + 1) % 4, zh)),
            "x-": (row, col_of(core, (x + 3) % 4, zh)),
            "zh+": (row, col_of(core, x, (zh + 1) % 4)),
            "zh-": (row, col_of(core, x, (zh + 3) % 4)),
            "core": (row, col_of(1 - core, x, zh)),
        }
        self.started = []

    def greet(self):
        barrier = pltpu.get_barrier_semaphore()
        for row, col in self.near.values():
            pl.semaphore_signal(barrier, inc=1, device_id={"row": row, "col": col}, device_id_type=MESH)
        return barrier

    def meet(self, barrier):
        pl.semaphore_wait(barrier, len(self.near))

    def copy(self, to, src, dst):
        row, col = self.near[to]
        k = len(self.started)
        out = pltpu.make_async_remote_copy(
            src_ref=src,
            dst_ref=dst,
            send_sem=self.send.at[k],
            recv_sem=self.recv.at[k],
            device_id={"row": row, "col": col},
            device_id_type=MESH,
        )
        out.start()
        self.started.append(out)
        return out

    def finish(self):
        for out in self.started:
            out.wait_send()


COPIES = 40


def gather_kernel(cv_ref, cb_ref, rv_ref, rb_ref, gc_ref, gr_ref, rn_ref, wc, gr, rn, last, send, recv, local):
    ring = Ring(send, recv)
    y, zl, core, x, zh = ring.y, ring.zl, ring.core, ring.x, ring.zh
    barrier = ring.greet()

    last[0:12, 0:L] = rv_ref[288:D].astype(F32)
    last[12:13, 0:L] = rb_ref[...].astype(F32)
    last[13:14, 0:L] = jnp.ones((1, L), F32)
    last[14:16, 0:L] = jnp.zeros((2, L), F32)
    gr[core, x, zh, 0:288] = rv_ref[0:288]
    gr[core, x, zh, 288:DP] = last[0:16, 0:L].astype(BF16)

    last[0:12, 0:SHARD] = cv_ref[288:D].astype(F32)
    last[12:13] = jnp.ones((1, (FULL + 1) * L), F32)
    last[13:14, 0:SHARD] = cb_ref[...].astype(F32)
    last[14:16] = jnp.zeros((2, (FULL + 1) * L), F32)
    shift = 32 * y
    lane = lax.broadcasted_iota(jnp.int32, (DP, L), 1)

    def turned(t):
        part = jnp.concatenate(
            [cv_ref[0:288, t * L : (t + 1) * L].astype(F32), last[0:16, t * L : (t + 1) * L]], axis=0
        )
        return pltpu.roll(part, shift, 1)

    before = first = turned(0)
    for t in range(1, FULL):
        part = turned(t)
        wc[t * DP : (t + 1) * DP] = jnp.where(lane < shift, before, part).astype(BF16)
        before = part
    wc[0:DP] = jnp.where(lane < shift, before, first).astype(BF16)
    part = jnp.concatenate(
        [cv_ref[0:288, FULL * L : SHARD].astype(F32), last[0:16, FULL * L : SHARD], jnp.zeros((4 * QR - DP, REST), F32)],
        axis=0,
    )
    part = jnp.concatenate([part, jnp.zeros((4 * QR, L - REST), F32)], axis=1)
    tail = part[:QR]
    for q in range(1, 4):
        tail = tail + pltpu.roll(part[q * QR : (q + 1) * QR], 32 * q, 1)
    wc[FULL * DP : PACK] = tail.astype(BF16)

    mine, other = row_of(y, zl), row_of(y, 1 - zl)
    up, down, far = row_of((y + 1) % 4, zl), row_of((y + 3) % 4, zl), row_of((y + 2) % 4, zl)
    xu, xd, xf = (x + 1) % 4, (x + 3) % 4, (x + 2) % 4
    own_c = pltpu.make_async_copy(wc, gc_ref.at[mine], local.at[0])
    own_c.start()
    outs = []

    def turn(c, xx):
        @pl.loop(0, 4)
        def _(z):
            rn[c, xx, z] = gr[c, xx, z].astype(F32).T.astype(BF16)

        for src, dst in ((gr, gr_ref), (rn, rn_ref)):
            out = pltpu.make_async_copy(src.at[c, xx], dst.at[c, xx], local.at[1 + len(outs)])
            out.start()
            outs.append(out)

    def own(to, c):
        return ring.copy(to, wc.at[chunk(c)], gc_ref.at[mine, chunk(c)])

    def pass_on(to, shard, c):
        part = gc_ref.at[shard, chunk(c)]
        return ring.copy(to, part, part)

    def rows(to, *at):
        part = gr.at[at]
        return ring.copy(to, part, part)

    ring.meet(barrier)
    r_z0 = rows("zh+", core, x, zh)
    r_z1 = rows("zh-", core, x, zh)
    c_u, c_d, c_z = {}, {}, {}
    for a, b in ((0, 2), (1, 3)):
        c_u[a], c_d[b] = own("y+", a), own("y-", b)
        c_z[a] = own("zl", a)
    c_z[2] = own("zl", 2)
    c_z[3] = own("zl", 3)

    r_z0.wait_recv()
    r_z2 = rows("zh+", core, x, (zh + 3) % 4, pl.ds(0, RHALF))
    r_z1.wait_recv()
    r_z3 = rows("zh-", core, x, (zh + 1) % 4, pl.ds(RHALF, DP - RHALF))

    f_u, f_d = {}, {}
    c_u[0].wait_recv()
    f_u[0] = pass_on("y+", down, 0)
    c_d[2].wait_recv()
    f_d[2] = pass_on("y-", up, 2)
    c_u[2], c_d[0] = own("y+", 2), own("y-", 0)

    r_z2.wait_recv()
    r_z3.wait_recv()
    r_x0 = rows("x+", core, x)
    r_x1 = rows("x-", core, x)
    r_c0 = rows("core", core, x)

    c_u[1].wait_recv()
    f_u[1] = pass_on("y+", down, 1)
    c_d[3].wait_recv()
    f_d[3] = pass_on("y-", up, 3)
    c_u[3], c_d[1] = own("y+", 3), own("y-", 1)

    turn(core, x)

    f_z = {}
    f_u[0].wait_recv()
    f_z[0] = pass_on("zl", far, 0)
    f_d[2].wait_recv()
    f_z[2] = pass_on("zl", far, 2)

    o_u, o_d = {}, {}
    c_z[0].wait_recv()
    o_u[0], o_d[0] = pass_on("y+", other, 0), pass_on("y-", other, 0)

    r_x0.wait_recv()
    r_x2 = rows("x+", core, xd, pl.ds(0, 2))
    r_c1 = rows("core", core, xd)
    r_x1.wait_recv()
    r_x3 = rows("x-", core, xu, pl.ds(2, 2))
    r_c2 = rows("core", core, xu)

    f_u[1].wait_recv()
    f_z[1] = pass_on("zl", far, 1)
    f_d[3].wait_recv()
    f_z[3] = pass_on("zl", far, 3)
    for c in (1, 2, 3):
        c_z[c].wait_recv()
        o_u[c], o_d[c] = pass_on("y+", other, c), pass_on("y-", other, c)

    turn(core, xd)
    turn(core, xu)
    r_x2.wait_recv()
    r_x3.wait_recv()
    r_c3 = rows("core", core, xf)
    turn(core, xf)
    for got, xx in ((r_c0, x), (r_c1, xd), (r_c2, xu), (r_c3, xf)):
        got.wait_recv()
        turn(1 - core, xx)

    rest = [c_u[2], c_u[3], c_d[0], c_d[1]]
    for c in range(4):
        rest += [o_u[c], o_d[c], f_z[c]]
    for got in rest:
        got.wait_recv()
    ring.finish()
    own_c.wait()
    for out in outs:
        out.wait()


def gather(cv, cb, rv, rb):
    return pl.pallas_call(
        gather_kernel,
        out_shape=(
            jax.ShapeDtypeStruct((SHARDS, PACK, L), BF16),
            jax.ShapeDtypeStruct((2, 4, 4, DP, L), BF16),
            jax.ShapeDtypeStruct((2, 4, 4, L, DP), BF16),
        ),
        in_specs=[IN_VMEM] * 4,
        out_specs=(ANY,) * 3,
        scratch_shapes=[
            pltpu.VMEM((PACK, L), BF16),
            pltpu.VMEM((2, 4, 4, DP, L), BF16),
            pltpu.VMEM((2, 4, 4, L, DP), BF16),
            pltpu.VMEM((16, (FULL + 1) * L), F32),
            pltpu.SemaphoreType.DMA((COPIES,)),
            pltpu.SemaphoreType.DMA((COPIES,)),
            pltpu.SemaphoreType.DMA((17,)),
        ],
        compiler_params=pltpu.CompilerParams(
            collective_id=0, has_side_effects=True, vmem_limit_bytes=VMEM_LIMIT
        ),
        name="gather",
    )(cv, cb, rv, rb)


def merge_tiles(ct):
    lane = lax.broadcasted_iota(jnp.int32, (DP, L), 1)

    def first(s):
        return ct[s * PACK : s * PACK + DP].astype(F32)

    def tail(s):
        part = ct[s * PACK + FULL * DP : (s + 1) * PACK].astype(F32)
        turns = [(32 * (s % 4) - 32 * q) % L for q in range(4)]
        return jnp.concatenate([pltpu.roll(part, n, 1) if n else part for n in turns], axis=0)[:DP]

    for quad in range(2):
        for k in (4, 3, 2, 1):
            s = quad * 4 + k
            tile = jnp.where(lane < 32 * k, tail(s - 1), first(s)) if k < 4 else tail(s - 1)
            if k > 1:
                tile = jnp.where(lane < 32 * (k - 1), first(s - 1), tile)
            at = s * PACK if k < 4 else SHARDS * PACK + quad * DP
            ct[at : at + DP] = tile.astype(BF16)


def tile_at(b):
    quad, j = b // QUAD, b % QUAD
    return jnp.where(j == QUAD - 1, SHARDS * PACK + quad * DP, (quad * 4 + j // FULL) * PACK + j % FULL * DP)


def pack_shard(tiles, s):
    k = s % 4
    base = (SHARD * s) // L
    lane = lax.broadcasted_iota(jnp.int32, (DP, L), 1)
    lane_q = lax.broadcasted_iota(jnp.int32, (QR, L), 1)
    after = tiles[base + FULL]
    head = tiles[base]
    if k:
        head = jnp.where(lane < 32 * k, after, head)
    parts = [(0, head)] + [(t * DP, tiles[base + t]) for t in range(1, FULL)]
    after = jnp.concatenate([after, jnp.zeros((4 * QR - DP, L), F32)], axis=0)
    tail = None
    for q in range(4):
        n = (32 * q - 32 * k) % L
        part = after[q * QR : (q + 1) * QR]
        part = pltpu.roll(part, n, 1) if n else part
        tail = part if q == 0 else jnp.where(lane_q < 32 * q, tail, part)
    return parts + [(FULL * DP, tail)]


LOG2_100 = 6.643856189774724
LN2 = 0.6931471805599453


def blocks_kernel(total_ref, rid_ref, cid_ref, counts_ref, gc_ref, gr_ref, rn_ref, pc_ref, pr_ref,
                  counts, ct, rt, rn, acc_c, acc_r, sems, count_sems):
    row, col = lax.axis_index("row"), lax.axis_index("col")
    total = total_ref[row, col]
    groups = (total + GROUP - 1) // GROUP
    loads = [
        pltpu.make_async_copy(gc_ref.at[s], ct.at[pl.ds(s * PACK, PACK)], sems.at[s]) for s in range(SHARDS)
    ]
    loads.append(pltpu.make_async_copy(rn_ref, rn, sems.at[8]))
    loads.append(pltpu.make_async_copy(gr_ref, rt, sems.at[9]))
    for one in loads:
        one.start()

    def load(g):
        part = pl.ds(g * GROUP, GROUP)
        return pltpu.make_async_copy(counts_ref.at[part], counts.at[part], count_sems.at[g])

    @pl.loop(0, groups)
    def _(g):
        load(g).start()

    @pl.loop(0, COL_TILES)
    def _(i):
        acc_c[i] = jnp.zeros((DP, L), F32)

    @pl.loop(0, ROW_TILES)
    def _(i):
        acc_r[i] = jnp.zeros((DP, L), F32)

    for one in loads[:8]:
        one.wait()
    merge_tiles(ct)
    for one in loads[8:]:
        one.wait()

    @pl.loop(0, groups)
    def _(g):
        load(g).wait()
        terms, rids, cids, tiles = [], [], [], []
        for k in range(GROUP):
            n = g * GROUP + k
            rid, cid = rid_ref[0, 0, n], cid_ref[0, 0, n]
            rid = rid % 2 * 16 + rid // 2 % 4 * 4 + rid // 8
            rids.append(rid)
            cids.append(cid)
            tile = pl.ds(pl.multiple_of(tile_at(cid), 16), DP)
            tiles.append(tile)
            scores = jnp.dot(rn[rid], ct[tile], preferred_element_type=F32)
            x = counts[n]
            least = jnp.where(n < total, 0, jnp.int32(2**31 - 1))
            log2x = jnp.log2(jnp.maximum(x.astype(F32), 1.0))
            weight2 = jnp.exp2(jnp.minimum(0.75 * log2x + (1.0 - 0.75 * LOG2_100), 1.0))
            term = weight2 * (scores - LN2 * log2x)
            terms.append(jnp.where(x > least, term, 0.0).astype(BF16))
        for k in range(GROUP):
            acc_c[cids[k]] += jnp.dot(rt[rids[k]], terms[k], preferred_element_type=F32)
            acc_r[rids[k]] += lax.dot_general(
                ct[tiles[k]], terms[k], (((1,), (1,)), ((), ())), preferred_element_type=F32
            )

    outs = [pltpu.make_async_copy(acc_r, pr_ref, sems.at[8])]
    outs[0].start()
    for s in range(SHARDS):
        for at, part in pack_shard(acc_c, s):
            ct[s * PACK + at : s * PACK + at + part.shape[0]] = part.astype(BF16)
        outs.append(pltpu.make_async_copy(ct.at[pl.ds(s * PACK, PACK)], pc_ref.at[s], sems.at[s]))
        outs[-1].start()
    for out in outs:
        out.wait()


def blocks(totals, rid, cid, counts, gc, gr, rn):
    return pl.pallas_call(
        blocks_kernel,
        out_shape=(
            jax.ShapeDtypeStruct((SHARDS, PACK, L), BF16),
            jax.ShapeDtypeStruct((ROW_TILES, DP, L), F32),
        ),
        in_specs=[IN_SMEM] * 3 + [ANY] * 4,
        out_specs=(ANY, ANY),
        scratch_shapes=[
            pltpu.VMEM((CAP, L, L), jnp.int32),
            pltpu.VMEM((SHARDS * PACK + 2 * DP, L), BF16),
            pltpu.VMEM((ROW_TILES, DP, L), BF16),
            pltpu.VMEM((ROW_TILES, L, DP), BF16),
            pltpu.VMEM((COL_TILES, DP, L), F32),
            pltpu.VMEM((ROW_TILES, DP, L), F32),
            pltpu.SemaphoreType.DMA((10,)),
            pltpu.SemaphoreType.DMA((CAP // GROUP,)),
        ],
        compiler_params=pltpu.CompilerParams(vmem_limit_bytes=VMEM_LIMIT),
        name="blocks",
    )(totals, rid, cid, counts, gc, gr, rn)


def reduce_kernel(pc_ref, pr_ref, oc_ref, or_ref,
                  pc, pr, got_c, half_c, put_c, got_core, got_x, put_x, half_x, half_z, got_z, put_z, u,
                  send, recv, local):
    ring = Ring(send, recv)
    y, zl, core, x, zh = ring.y, ring.zl, ring.core, ring.x, ring.zh
    zo = 1 - zl
    barrier = ring.greet()
    up, down, far = (y + 1) % 4, (y + 3) % 4, (y + 2) % 4
    xu, xd, xf = (x + 1) % 4, (x + 3) % 4, (x + 2) % 4
    zu, zd, zf = (zh + 1) % 4, (zh + 3) % 4, (zh + 2) % 4
    FAR, OTHER, UP, DOWN, MINE = range(5)
    wanted = (row_of(far, zl), row_of(y, zo), row_of(up, zl), row_of(down, zl), row_of(y, zl))
    loads = [pltpu.make_async_copy(pc_ref.at[w], pc.at[i], local.at[i]) for i, w in enumerate(wanted)]
    load_r = pltpu.make_async_copy(pr_ref.at[core], pr, local.at[5])
    loads[FAR].start()
    load_r.start()
    for k in range(1, 5):
        loads[k].start()
    ring.meet(barrier)

    def raw(to, y_to, c, k):
        return ring.copy(to, pc_ref.at[row_of(y_to, zo), chunk(c)], got_c.at[k, chunk(c)])

    def put(to, k, c, dst):
        return ring.copy(to, put_c.at[k, chunk(c)], dst.at[chunk(c)])

    def total(k, c, *more):
        at = chunk(c)
        out = pc[k, at].astype(F32)
        for one in more:
            out = out + one[at].astype(F32)
        return out

    a_z, a_u, a_d = {}, {}, {}
    for c in (0, 1):
        a_z[2 * c] = raw("zl", far, 2 * c, 0)
        a_u[c], a_d[c] = raw("y+", up, c, 1), raw("y-", down, c, 2)
    for c in (1, 3):
        a_z[c] = raw("zl", far, c, 0)
    b_c = [ring.copy("core", pr_ref.at[1 - core, w], got_core.at[k]) for k, w in enumerate((xf, xu, xd, x))]
    for one in loads:
        one.wait()
    load_r.wait()

    q2 = {}

    def pass_far(c):
        a_z[c].wait_recv()
        put_c[0, chunk(c)] = total(FAR, c, got_c.at[0]).astype(BF16)
        q2[c] = put("y+" if c < 2 else "y-", 0, c, half_c)

    qz = {}

    def pass_other(c):
        a_u[c].wait_recv()
        a_d[c].wait_recv()
        put_c[1, chunk(c)] = total(OTHER, c, got_c.at[1], got_c.at[2]).astype(BF16)
        qz[c] = put("zl", 1, c, got_c.at[3])

    q_u, q_d = {}, {}

    def pass_near(c):
        q2[c].wait_recv()
        if c < 2:
            put_c[2, chunk(c)] = total(UP, c, half_c).astype(BF16)
            q_u[c] = put("y+", 2, c, got_c.at[4])
        else:
            put_c[2, chunk(c)] = total(DOWN, c, half_c).astype(BF16)
            q_d[c] = put("y-", 2, c, got_c.at[5])

    def pass_plain(c):
        if c < 2:
            q_d[c] = ring.copy("y-", pc.at[DOWN, chunk(c)], got_c.at[5, chunk(c)])
        else:
            q_u[c] = ring.copy("y+", pc.at[UP, chunk(c)], got_c.at[4, chunk(c)])

    pass_far(0)
    a_u[2], a_d[2] = raw("y+", up, 2, 1), raw("y-", down, 2, 2)
    b_c[0].wait_recv()
    for z in range(4):
        put_x[0, z] = (pr[xf, z] + got_core[0, z]).astype(BF16)
    b_x0 = ring.copy("x+", put_x.at[0, pl.ds(0, 2)], half_x.at[0])
    b_x1 = ring.copy("x-", put_x.at[0, pl.ds(2, 2)], half_x.at[1])
    pass_far(2)
    a_u[3], a_d[3] = raw("y+", up, 3, 1), raw("y-", down, 3, 2)
    pass_other(0)
    pass_far(1)
    pass_other(1)

    b_c[1].wait_recv()
    b_x0.wait_recv()
    for z in range(4):
        one = pr[xu, z] + got_core[1, z]
        if z < 2:
            one = one + half_x[0, z].astype(F32)
        put_x[1, z] = one.astype(BF16)
    b_x2 = ring.copy("x+", put_x.at[1], got_x.at[0])
    b_c[2].wait_recv()
    b_x1.wait_recv()
    for z in range(4):
        one = pr[xd, z] + got_core[2, z]
        if z >= 2:
            one = one + half_x[1, z - 2].astype(F32)
        put_x[2, z] = one.astype(BF16)
    b_x3 = ring.copy("x-", put_x.at[2], got_x.at[1])

    pass_far(3)
    pass_plain(0)
    pass_plain(2)
    pass_near(0)
    pass_near(2)
    pass_other(2)
    pass_plain(1)
    pass_plain(3)
    pass_near(1)
    pass_near(3)
    pass_other(3)

    b_c[3].wait_recv()
    b_x2.wait_recv()
    b_x3.wait_recv()
    for z in range(4):
        u[z] = pr[x, z] + got_core[3, z] + got_x[0, z].astype(F32) + got_x[1, z].astype(F32)
    put_z[0] = u[zf].astype(BF16)
    rlo, rhi = pl.ds(0, RHALF), pl.ds(RHALF, DP - RHALF)
    b_z0 = ring.copy("zh+", put_z.at[0, rlo], half_z.at[rlo])
    b_z1 = ring.copy("zh-", put_z.at[0, rhi], half_z.at[rhi])
    b_z0.wait_recv()
    put_z[1, 0:RHALF] = (u[zu, 0:RHALF] + half_z[0:RHALF].astype(F32)).astype(BF16)
    put_z[1, RHALF:DP] = u[zu, RHALF:DP].astype(BF16)
    b_z2 = ring.copy("zh+", put_z.at[1], got_z.at[0])
    b_z1.wait_recv()
    put_z[2, 0:RHALF] = u[zd, 0:RHALF].astype(BF16)
    put_z[2, RHALF:DP] = (u[zd, RHALF:DP] + half_z[RHALF:DP].astype(F32)).astype(BF16)
    b_z3 = ring.copy("zh-", put_z.at[2], got_z.at[1])

    for c in range(4):
        for got in (qz, q_u, q_d):
            got[c].wait_recv()

    def col_sum(start, size):
        at = pl.ds(start, size)
        return (
            pc[MINE, at].astype(F32) + got_c[3, at].astype(F32)
            + got_c[4, at].astype(F32) + got_c[5, at].astype(F32)
        )

    shift = 32 * y
    back = (L - shift) % L
    lane = lax.broadcasted_iota(jnp.int32, (DP, L), 1)
    sums = [col_sum(t * DP, DP) for t in range(FULL)]
    for t in range(FULL):
        oc_ref[:, t * L : (t + 1) * L] = pltpu.roll(
            jnp.where(lane < shift, sums[(t + 1) % FULL], sums[t]), back, 1
        )
    tail = col_sum(FULL * DP, QR)
    for q in range(4):
        part = pltpu.roll(tail, L - 32 * q, 1) if q else tail
        rows = min(QR, DP - q * QR)
        oc_ref[q * QR : q * QR + rows, FULL * L :] = part[:rows]

    b_z2.wait_recv()
    b_z3.wait_recv()
    or_ref[...] = u[zh] + got_z[0].astype(F32) + got_z[1].astype(F32)
    ring.finish()


def reduce(pc, pr):
    return pl.pallas_call(
        reduce_kernel,
        out_shape=(
            jax.ShapeDtypeStruct((DP, (FULL + 1) * L), F32),
            jax.ShapeDtypeStruct((DP, L), F32),
        ),
        in_specs=[ANY, ANY],
        out_specs=(IN_VMEM,) * 2,
        scratch_shapes=[
            pltpu.VMEM((5, PACK, L), BF16),
            pltpu.VMEM((4, 4, DP, L), F32),
            pltpu.VMEM((6, PACK, L), BF16),
            pltpu.VMEM((PACK, L), BF16),
            pltpu.VMEM((3, PACK, L), BF16),
            pltpu.VMEM((4, 4, DP, L), F32),
            pltpu.VMEM((2, 4, DP, L), BF16),
            pltpu.VMEM((3, 4, DP, L), BF16),
            pltpu.VMEM((2, 2, DP, L), BF16),
            pltpu.VMEM((DP, L), BF16),
            pltpu.VMEM((2, DP, L), BF16),
            pltpu.VMEM((3, DP, L), BF16),
            pltpu.VMEM((4, DP, L), F32),
            pltpu.SemaphoreType.DMA((COPIES,)),
            pltpu.SemaphoreType.DMA((COPIES,)),
            pltpu.SemaphoreType.DMA((6,)),
        ],
        compiler_params=pltpu.CompilerParams(
            collective_id=1, has_side_effects=True, vmem_limit_bytes=VMEM_LIMIT
        ),
        name="reduce",
    )(pc, pr)


def outputs_kernel(oc_ref, or_ref, row_ref, row_bias_ref, col_ref, col_bias_ref):
    col_ref[...] = oc_ref[:D, :SHARD]
    col_bias_ref[...] = oc_ref[D + 1, :SHARD]
    row_ref[...] = or_ref[:D]
    row_bias_ref[...] = or_ref[D]


def outputs(oc, orow):
    return pl.pallas_call(
        outputs_kernel,
        out_shape=(
            jax.ShapeDtypeStruct((D, L), F32),
            jax.ShapeDtypeStruct((L,), F32),
            jax.ShapeDtypeStruct((D, SHARD), F32),
            jax.ShapeDtypeStruct((SHARD,), F32),
        ),
        in_specs=[IN_VMEM] * 2,
        out_specs=(IN_VMEM,) * 4,
        name="outputs",
    )(oc, orow)


def body(row_vecs, row_bias, col_vecs, col_bias, row_block, col_block, counts, block_totals):
    gc, gr, rn = gather(col_vecs.T, col_bias[None], row_vecs.T, row_bias[None])
    pc, pr = blocks(
        block_totals, row_block, col_block, counts.reshape(CAP, L, L), gc,
        gr.reshape(ROW_TILES, DP, L), rn.reshape(ROW_TILES, L, DP),
    )
    grad_rows, grad_row_bias, grad_cols, grad_col_bias = outputs(*reduce(pc, pr.reshape(2, 4, 4, DP, L)))
    return grad_rows.T, grad_row_bias, grad_cols.T, grad_col_bias


def solution(mesh):
    placed = (
        P(("row", "col"), None),
        P(("row", "col")),
        P(("col", "row"), None),
        P(("col", "row")),
        P("row", "col", None),
        P("row", "col", None),
        P("row", "col", None, None, None),
        P(),
    )
    return jax.shard_map(
        body,
        mesh=mesh,
        in_specs=placed,
        out_specs=(
            P(("row", "col"), None),
            P(("row", "col")),
            P(("col", "row"), None),
            P(("col", "row")),
        ),
        check_vma=False,
    )
```

time: 129 us -> 111 us (0.86)
  the two profiles are of different devices: /device:TPU:66 before, /device:TPU:1 now
where the time goes in v2:
time: 111 us
  Pallas kernels  109 us (98%)
  local copies, waits for them, and re-layouts  1.26 us (1%)
    pallas_call x1, Pallas kernels, gather(): pl.pallas_call(gather_kernel, out_shape=(jax.ShapeDtypeStruct((SHARDS, PA...  45.2 us
    pallas_call x1, Pallas kernels, reduce(): pl.pallas_call(reduce_kernel, out_shape=(jax.ShapeDtypeStruct((DP, (FULL...  45.1 us
    pallas_call x1, Pallas kernels, blocks(): pl.pallas_call(blocks_kernel, out_shape=(jax.ShapeDtypeStruct((SHARDS, PA...  16.2 us
    pallas_call x1, Pallas kernels, outputs(): pl.pallas_call(outputs_kernel, out_shape=(jax.ShapeDtypeStruct((D, L), F3...  2.34 us

profile of v2, /device:TPU:1, one launch (start us, length us, event | category | flops | bytes accessed | tf_op | source)
XLA Modules:
  0.0 110.8 jit_solution(17615060431102181015)
XLA Ops:
  0.6 1.3 %broadcast_in_dim.6.cb_ref = bf16[1,800]{1,0:T(2,128)(2,1)} reshape(bf16[800]{0:T(1024)(128)(2,1)} %param.11) | data formatting | bytes 3200 | tf_op jit(solution)/shard_map/broadcast_in_dim | solution.py:648
  1.9 45.2 %gather.1 = (bf16[8,1904,128]{2,1,0:T(8,128)(2,1)}, bf16[2,4,4,304,128]{4,3,2,1,0:T(8,128)(2,1)}, bf16[2,4,4,128,304]{4,3,2,1,0:T(8,128)(2,1)}) custom-call(bf16[300,800]{1,0:T(8,128)(2,1)} %bitcast.13, bf16[1,800]{1,0:T(2,128)(2,1)} %broadcast_in_dim.6.cb_ref, bf16[300,128]{1,0:T(8,128)(2,1)} %bitcast.14, bf16[1,128]{1,0:T(2,128)(2,1)} %bitcast.15), custom_call_target="tpu_custom_call" | custom-call | tf_op jit(solution)/shard_map/gather/pallas_call | solution.py:254
  47.1 16.2 %blocks.1 = (bf16[8,1904,128]{2,1,0:T(8,128)(2,1)}, f32[32,304,128]{2,1,0:T(8,128)}) custom-call(s32[8,32]{1,0:T(8,128)} %total_ref.1, s32[1,1,128]{2,1,0:T(1,128)} %rid_ref.1, s32[1,1,128]{2,1,0:T(1,128)} %cid_ref.1, s32[128,128,128]{2,1,0:T(8,128)} %bitcast.9, bf16[8,1904,128]{2,1,0:T(8,128)(2,1)} %get-tuple-element.15.gc_ref, ...), custom_call_target="tpu_custom_call" | custom-call | tf_op jit(solution)/shard_map/blocks/pallas_call | solution.py:401
  63.3 45.1 %reduce.1 = (f32[304,896]{1,0:T(8,128)}, f32[304,128]{1,0:T(8,128)}) custom-call(bf16[8,1904,128]{2,1,0:T(8,128)(2,1)} %get-tuple-element.18.pc_ref, f32[2,4,4,304,128]{4,3,2,1,0:T(8,128)} %bitcast.10), custom_call_target="tpu_custom_call" | custom-call | tf_op jit(solution)/shard_map/reduce/pallas_call | solution.py:592
  108.4 2.3 %outputs.1 = (f32[300,128]{1,0:T(8,128)}, f32[128]{0:T(128)}, f32[300,800]{1,0:T(8,128)}, f32[800]{0:T(1024)}) custom-call(f32[304,896]{1,0:T(8,128)} %get-tuple-element.20.oc_ref, f32[304,128]{1,0:T(8,128)} %get-tuple-element.21.or_ref), custom_call_target="tpu_custom_call" | custom-call | tf_op jit(solution)/shard_map/outputs/pallas_call | solution.py:633

commit v3 on v2

--- a/solution.py
+++ b/solution.py
@@ -6,7 +6,7 @@
 from jax.sharding import PartitionSpec as P
 
 MESH = pl.DeviceIdType.MESH
-ANY = pl.BlockSpec(memory_space=pl.ANY)
+IN_HBM = pl.BlockSpec(memory_space=pltpu.HBM)
 IN_VMEM = pl.BlockSpec(memory_space=pltpu.VMEM)
 IN_SMEM = pl.BlockSpec(memory_space=pltpu.SMEM)
 F32, BF16 = jnp.float32, jnp.bfloat16
@@ -26,8 +26,9 @@
 COL_TILES = 50
 QUAD = COL_TILES // 2
 CAP = 128
-GROUP = 8
-VMEM_LIMIT = 56 * 1024 * 1024
+TILES = SHARDS * PACK + 8 * DP
+GROUP = 16
+MIB = 1024 * 1024
 
 
 def chunk(c):
@@ -96,24 +97,33 @@
             out.wait_send()
 
 
-COPIES = 40
-
-
-def gather_kernel(cv_ref, cb_ref, rv_ref, rb_ref, gc_ref, gr_ref, rn_ref, wc, gr, rn, last, send, recv, local):
+COPIES = 48
+
+
+def gather_kernel(cv_hbm, cb_hbm, rv_hbm, rb_hbm, counts_hbm, gc, gr, rn, counts,
+                  cv_ref, cb_ref, rv_ref, rb_ref, wc, last, send, recv, local):
+    pairs = ((rv_hbm, rv_ref), (rb_hbm, rb_ref), (cv_hbm, cv_ref), (cb_hbm, cb_ref), (counts_hbm, counts))
+    loads = [pltpu.make_async_copy(src, dst, local.at[1 + k]) for k, (src, dst) in enumerate(pairs)]
+    for load in loads:
+        load.start()
     ring = Ring(send, recv)
     y, zl, core, x, zh = ring.y, ring.zl, ring.core, ring.x, ring.zh
     barrier = ring.greet()
 
+    for load in loads[:2]:
+        load.wait()
     last[0:12, 0:L] = rv_ref[288:D].astype(F32)
-    last[12:13, 0:L] = rb_ref[...].astype(F32)
+    last[12:13, 0:L] = rb_ref[...].astype(F32).reshape(1, L)
     last[13:14, 0:L] = jnp.ones((1, L), F32)
     last[14:16, 0:L] = jnp.zeros((2, L), F32)
     gr[core, x, zh, 0:288] = rv_ref[0:288]
     gr[core, x, zh, 288:DP] = last[0:16, 0:L].astype(BF16)
 
+    for load in loads[2:4]:
+        load.wait()
     last[0:12, 0:SHARD] = cv_ref[288:D].astype(F32)
     last[12:13] = jnp.ones((1, (FULL + 1) * L), F32)
-    last[13:14, 0:SHARD] = cb_ref[...].astype(F32)
+    last[13:14, 0:SHARD] = cb_ref[...].astype(F32).reshape(1, SHARD)
     last[14:16] = jnp.zeros((2, (FULL + 1) * L), F32)
     shift = 32 * y
     lane = lax.broadcasted_iota(jnp.int32, (DP, L), 1)
@@ -143,99 +153,104 @@
     mine, other = row_of(y, zl), row_of(y, 1 - zl)
     up, down, far = row_of((y + 1) % 4, zl), row_of((y + 3) % 4, zl), row_of((y + 2) % 4, zl)
     xu, xd, xf = (x + 1) % 4, (x + 3) % 4, (x + 2) % 4
-    own_c = pltpu.make_async_copy(wc, gc_ref.at[mine], local.at[0])
+    own_c = pltpu.make_async_copy(wc, gc.at[pl.ds(mine * PACK, PACK)], local.at[0])
     own_c.start()
-    outs = []
 
     def turn(c, xx):
         @pl.loop(0, 4)
         def _(z):
             rn[c, xx, z] = gr[c, xx, z].astype(F32).T.astype(BF16)
 
-        for src, dst in ((gr, gr_ref), (rn, rn_ref)):
-            out = pltpu.make_async_copy(src.at[c, xx], dst.at[c, xx], local.at[1 + len(outs)])
-            out.start()
-            outs.append(out)
+    def part_of(shard, c):
+        return gc.at[pl.ds(pl.multiple_of(shard * PACK + CUTS[c], 16), CUTS[c + 1] - CUTS[c])]
 
     def own(to, c):
-        return ring.copy(to, wc.at[chunk(c)], gc_ref.at[mine, chunk(c)])
+        return ring.copy(to, wc.at[chunk(c)], part_of(mine, c))
 
     def pass_on(to, shard, c):
-        part = gc_ref.at[shard, chunk(c)]
-        return ring.copy(to, part, part)
+        return ring.copy(to, part_of(shard, c), part_of(shard, c))
 
     def rows(to, *at):
-        part = gr.at[at]
-        return ring.copy(to, part, part)
-
+        return ring.copy(to, gr.at[at], gr.at[at])
+
+    zu, zd, zf = (zh + 1) % 4, (zh + 3) % 4, (zh + 2) % 4
     ring.meet(barrier)
-    r_z0 = rows("zh+", core, x, zh)
-    r_z1 = rows("zh-", core, x, zh)
+    r_zu = rows("zh+", core, x, zh)
+    r_zd = rows("zh-", core, x, zh)
+    x_u, x_d, x_f = {}, {}, {}
+    x_u["own"], x_d["own"] = rows("x+", core, x, zh), rows("x-", core, x, zh)
     c_u, c_d, c_z = {}, {}, {}
     for a, b in ((0, 2), (1, 3)):
         c_u[a], c_d[b] = own("y+", a), own("y-", b)
         c_z[a] = own("zl", a)
-    c_z[2] = own("zl", 2)
-    c_z[3] = own("zl", 3)
-
-    r_z0.wait_recv()
-    r_z2 = rows("zh+", core, x, (zh + 3) % 4, pl.ds(0, RHALF))
-    r_z1.wait_recv()
-    r_z3 = rows("zh-", core, x, (zh + 1) % 4, pl.ds(RHALF, DP - RHALF))
-
-    f_u, f_d = {}, {}
+
+    f_u, f_d, f_z, o_u, o_d = {}, {}, {}, {}, {}
     c_u[0].wait_recv()
     f_u[0] = pass_on("y+", down, 0)
     c_d[2].wait_recv()
     f_d[2] = pass_on("y-", up, 2)
     c_u[2], c_d[0] = own("y+", 2), own("y-", 0)
-
-    r_z2.wait_recv()
-    r_z3.wait_recv()
-    r_x0 = rows("x+", core, x)
-    r_x1 = rows("x-", core, x)
-    r_c0 = rows("core", core, x)
+    c_z[2] = own("zl", 2)
+
+    r_zu.wait_recv()
+    r_fu = rows("zh+", core, x, zd, pl.ds(0, RHALF))
+    x_u["zd"], x_d["zd"] = rows("x+", core, x, zd), rows("x-", core, x, zd)
+    r_zd.wait_recv()
+    r_fd = rows("zh-", core, x, zu, pl.ds(RHALF, DP - RHALF))
+    x_u["zu"], x_d["zu"] = rows("x+", core, x, zu), rows("x-", core, x, zu)
 
     c_u[1].wait_recv()
     f_u[1] = pass_on("y+", down, 1)
     c_d[3].wait_recv()
     f_d[3] = pass_on("y-", up, 3)
     c_u[3], c_d[1] = own("y+", 3), own("y-", 1)
-
-    turn(core, x)
-
-    f_z = {}
+    c_z[3] = own("zl", 3)
+
+    x_u["own"].wait_recv()
+    x_f["own"] = rows("x+", core, xd, zh)
+
     f_u[0].wait_recv()
     f_z[0] = pass_on("zl", far, 0)
     f_d[2].wait_recv()
     f_z[2] = pass_on("zl", far, 2)
 
-    o_u, o_d = {}, {}
+    r_fu.wait_recv()
+    r_fd.wait_recv()
+    x_u["zf"], x_d["zf"] = rows("x+", core, x, zf), rows("x-", core, x, zf)
+    x_d["zd"].wait_recv()
+    x_f["zd"] = rows("x-", core, xu, zd)
+    x_u["zu"].wait_recv()
+    x_f["zu"] = rows("x+", core, xd, zu)
     c_z[0].wait_recv()
     o_u[0], o_d[0] = pass_on("y+", other, 0), pass_on("y-", other, 0)
-
-    r_x0.wait_recv()
-    r_x2 = rows("x+", core, xd, pl.ds(0, 2))
-    r_c1 = rows("core", core, xd)
-    r_x1.wait_recv()
-    r_x3 = rows("x-", core, xu, pl.ds(2, 2))
-    r_c2 = rows("core", core, xu)
 
     f_u[1].wait_recv()
     f_z[1] = pass_on("zl", far, 1)
     f_d[3].wait_recv()
     f_z[3] = pass_on("zl", far, 3)
-    for c in (1, 2, 3):
+    k_own = rows("core", core, x)
+    for c in (1, 2):
         c_z[c].wait_recv()
         o_u[c], o_d[c] = pass_on("y+", other, c), pass_on("y-", other, c)
 
-    turn(core, xd)
-    turn(core, xu)
-    r_x2.wait_recv()
-    r_x3.wait_recv()
-    r_c3 = rows("core", core, xf)
-    turn(core, xf)
-    for got, xx in ((r_c0, x), (r_c1, xd), (r_c2, xu), (r_c3, xf)):
+    x_d["zf"].wait_recv()
+    x_f["zf"] = rows("x-", core, xu, zf)
+    for one in (x_d["own"], x_d["zu"]):
+        one.wait_recv()
+    k_up = rows("core", core, xu)
+    for one in (x_u["zd"], x_u["zf"]):
+        one.wait_recv()
+    k_down = rows("core", core, xd)
+    c_z[3].wait_recv()
+    o_u[3], o_d[3] = pass_on("y+", other, 3), pass_on("y-", other, 3)
+
+    turn(core, x)
+    for one in x_f.values():
+        one.wait_recv()
+    k_far = rows("core", core, xf)
+    for xx in (xd, xu, xf):
+        turn(core, xx)
+    for got, xx in ((k_own, x), (k_up, xu), (k_down, xd), (k_far, xf)):
         got.wait_recv()
         turn(1 - core, xx)
 
@@ -244,36 +259,39 @@
         rest += [o_u[c], o_d[c], f_z[c]]
     for got in rest:
         got.wait_recv()
+    own_c.wait()
+    merge_tiles(gc)
     ring.finish()
-    own_c.wait()
-    for out in outs:
-        out.wait()
-
-
-def gather(cv, cb, rv, rb):
+    loads[4].wait()
+
+
+def gather(cv, cb, rv, rb, counts):
     return pl.pallas_call(
         gather_kernel,
         out_shape=(
-            jax.ShapeDtypeStruct((SHARDS, PACK, L), BF16),
-            jax.ShapeDtypeStruct((2, 4, 4, DP, L), BF16),
-            jax.ShapeDtypeStruct((2, 4, 4, L, DP), BF16),
-        ),
-        in_specs=[IN_VMEM] * 4,
-        out_specs=(ANY,) * 3,
-        scratch_shapes=[
-            pltpu.VMEM((PACK, L), BF16),
+            pltpu.VMEM((TILES, L), BF16),
             pltpu.VMEM((2, 4, 4, DP, L), BF16),
             pltpu.VMEM((2, 4, 4, L, DP), BF16),
+            pltpu.VMEM((CAP, L, L), jnp.int32),
+        ),
+        in_specs=[IN_HBM] * 5,
+        out_specs=(IN_VMEM,) * 4,
+        scratch_shapes=[
+            pltpu.VMEM((D, SHARD), BF16),
+            pltpu.VMEM((SHARD,), BF16),
+            pltpu.VMEM((D, L), BF16),
+            pltpu.VMEM((L,), BF16),
+            pltpu.VMEM((PACK, L), BF16),
             pltpu.VMEM((16, (FULL + 1) * L), F32),
             pltpu.SemaphoreType.DMA((COPIES,)),
             pltpu.SemaphoreType.DMA((COPIES,)),
-            pltpu.SemaphoreType.DMA((17,)),
+            pltpu.SemaphoreType.DMA((6,)),
         ],
         compiler_params=pltpu.CompilerParams(
-            collective_id=0, has_side_effects=True, vmem_limit_bytes=VMEM_LIMIT
+            collective_id=0, has_side_effects=True, vmem_limit_bytes=8 * MIB
         ),
         name="gather",
-    )(cv, cb, rv, rb)
+    )(*(pltpu.with_memory_space_constraint(a, pltpu.HBM) for a in (cv, cb, rv, rb, counts)))
 
 
 def merge_tiles(ct):
@@ -287,19 +305,22 @@
         turns = [(32 * (s % 4) - 32 * q) % L for q in range(4)]
         return jnp.concatenate([pltpu.roll(part, n, 1) if n else part for n in turns], axis=0)[:DP]
 
-    for quad in range(2):
-        for k in (4, 3, 2, 1):
-            s = quad * 4 + k
-            tile = jnp.where(lane < 32 * k, tail(s - 1), first(s)) if k < 4 else tail(s - 1)
-            if k > 1:
-                tile = jnp.where(lane < 32 * (k - 1), first(s - 1), tile)
-            at = s * PACK if k < 4 else SHARDS * PACK + quad * DP
-            ct[at : at + DP] = tile.astype(BF16)
+    for s in range(SHARDS):
+        k = s % 4
+        tile = tail(s)
+        if k:
+            tile = jnp.where(lane < 32 * k, first(s), tile)
+        if k < 3:
+            tile = jnp.where(lane < 32 * (k + 1), tile, first(s + 1))
+        at = SHARDS * PACK + s * DP
+        ct[at : at + DP] = tile.astype(BF16)
 
 
 def tile_at(b):
     quad, j = b // QUAD, b % QUAD
-    return jnp.where(j == QUAD - 1, SHARDS * PACK + quad * DP, (quad * 4 + j // FULL) * PACK + j % FULL * DP)
+    k, t = j // FULL, j % FULL
+    shared = (k > 0) & (t == 0)
+    return jnp.where(shared, SHARDS * PACK + (quad * 4 + k - 1) * DP, (quad * 4 + k) * PACK + t * DP)
 
 
 def pack_shard(tiles, s):
@@ -326,26 +347,10 @@
 LN2 = 0.6931471805599453
 
 
-def blocks_kernel(total_ref, rid_ref, cid_ref, counts_ref, gc_ref, gr_ref, rn_ref, pc_ref, pr_ref,
-                  counts, ct, rt, rn, acc_c, acc_r, sems, count_sems):
+def blocks_kernel(total_ref, rid_ref, cid_ref, counts, ct, rt, rn, pc, acc_r, acc_c):
     row, col = lax.axis_index("row"), lax.axis_index("col")
     total = total_ref[row, col]
     groups = (total + GROUP - 1) // GROUP
-    loads = [
-        pltpu.make_async_copy(gc_ref.at[s], ct.at[pl.ds(s * PACK, PACK)], sems.at[s]) for s in range(SHARDS)
-    ]
-    loads.append(pltpu.make_async_copy(rn_ref, rn, sems.at[8]))
-    loads.append(pltpu.make_async_copy(gr_ref, rt, sems.at[9]))
-    for one in loads:
-        one.start()
-
-    def load(g):
-        part = pl.ds(g * GROUP, GROUP)
-        return pltpu.make_async_copy(counts_ref.at[part], counts.at[part], count_sems.at[g])
-
-    @pl.loop(0, groups)
-    def _(g):
-        load(g).start()
 
     @pl.loop(0, COL_TILES)
     def _(i):
@@ -355,15 +360,8 @@
     def _(i):
         acc_r[i] = jnp.zeros((DP, L), F32)
 
-    for one in loads[:8]:
-        one.wait()
-    merge_tiles(ct)
-    for one in loads[8:]:
-        one.wait()
-
     @pl.loop(0, groups)
     def _(g):
-        load(g).wait()
         terms, rids, cids, tiles = [], [], [], []
         for k in range(GROUP):
             n = g * GROUP + k
@@ -381,49 +379,38 @@
             term = weight2 * (scores - LN2 * log2x)
             terms.append(jnp.where(x > least, term, 0.0).astype(BF16))
         for k in range(GROUP):
-            acc_c[cids[k]] += jnp.dot(rt[rids[k]], terms[k], preferred_element_type=F32)
-            acc_r[rids[k]] += lax.dot_general(
-                ct[tiles[k]], terms[k], (((1,), (1,)), ((), ())), preferred_element_type=F32
+            term, none = terms[k], jnp.zeros((L, L), BF16)
+            both = jnp.concatenate(
+                [jnp.concatenate([term, none], axis=1), jnp.concatenate([none, term.T], axis=1)], axis=0
             )
-
-    outs = [pltpu.make_async_copy(acc_r, pr_ref, sems.at[8])]
-    outs[0].start()
+            vecs = jnp.concatenate([rt[rids[k]], ct[tiles[k]]], axis=1)
+            grads = jnp.dot(vecs, both, preferred_element_type=F32)
+            acc_c[cids[k]] += grads[:, :L]
+            acc_r[rids[k]] += grads[:, L:]
+
     for s in range(SHARDS):
         for at, part in pack_shard(acc_c, s):
-            ct[s * PACK + at : s * PACK + at + part.shape[0]] = part.astype(BF16)
-        outs.append(pltpu.make_async_copy(ct.at[pl.ds(s * PACK, PACK)], pc_ref.at[s], sems.at[s]))
-        outs[-1].start()
-    for out in outs:
-        out.wait()
+            pc[s, at : at + part.shape[0]] = part.astype(BF16)
 
 
 def blocks(totals, rid, cid, counts, gc, gr, rn):
     return pl.pallas_call(
         blocks_kernel,
         out_shape=(
-            jax.ShapeDtypeStruct((SHARDS, PACK, L), BF16),
-            jax.ShapeDtypeStruct((ROW_TILES, DP, L), F32),
+            pltpu.VMEM((SHARDS, PACK, L), BF16),
+            pltpu.VMEM((ROW_TILES, DP, L), F32),
         ),
-        in_specs=[IN_SMEM] * 3 + [ANY] * 4,
-        out_specs=(ANY, ANY),
-        scratch_shapes=[
-            pltpu.VMEM((CAP, L, L), jnp.int32),
-            pltpu.VMEM((SHARDS * PACK + 2 * DP, L), BF16),
-            pltpu.VMEM((ROW_TILES, DP, L), BF16),
-            pltpu.VMEM((ROW_TILES, L, DP), BF16),
-            pltpu.VMEM((COL_TILES, DP, L), F32),
-            pltpu.VMEM((ROW_TILES, DP, L), F32),
-            pltpu.SemaphoreType.DMA((10,)),
-            pltpu.SemaphoreType.DMA((CAP // GROUP,)),
-        ],
-        compiler_params=pltpu.CompilerParams(vmem_limit_bytes=VMEM_LIMIT),
+        in_specs=[IN_SMEM] * 3 + [IN_VMEM] * 4,
+        out_specs=(IN_VMEM, IN_VMEM),
+        scratch_shapes=[pltpu.VMEM((COL_TILES, DP, L), F32)],
+        compiler_params=pltpu.CompilerParams(vmem_limit_bytes=14 * MIB),
         name="blocks",
     )(totals, rid, cid, counts, gc, gr, rn)
 
 
 def reduce_kernel(pc_ref, pr_ref, oc_ref, or_ref,
-                  pc, pr, got_c, half_c, put_c, got_core, got_x, put_x, half_x, half_z, got_z, put_z, u,
-                  send, recv, local):
+                  got_c, half_c, put_c, got_core, got_x, put_x, half_x, half_z, got_z, put_z, u,
+                  send, recv):
     ring = Ring(send, recv)
     y, zl, core, x, zh = ring.y, ring.zl, ring.core, ring.x, ring.zh
     zo = 1 - zl
@@ -433,12 +420,7 @@
     zu, zd, zf = (zh + 1) % 4, (zh + 3) % 4, (zh + 2) % 4
     FAR, OTHER, UP, DOWN, MINE = range(5)
     wanted = (row_of(far, zl), row_of(y, zo), row_of(up, zl), row_of(down, zl), row_of(y, zl))
-    loads = [pltpu.make_async_copy(pc_ref.at[w], pc.at[i], local.at[i]) for i, w in enumerate(wanted)]
-    load_r = pltpu.make_async_copy(pr_ref.at[core], pr, local.at[5])
-    loads[FAR].start()
-    load_r.start()
-    for k in range(1, 5):
-        loads[k].start()
+    pr = pr_ref.at[core]
     ring.meet(barrier)
 
     def raw(to, y_to, c, k):
@@ -449,7 +431,7 @@
 
     def total(k, c, *more):
         at = chunk(c)
-        out = pc[k, at].astype(F32)
+        out = pc_ref[wanted[k], at].astype(F32)
         for one in more:
             out = out + one[at].astype(F32)
         return out
@@ -461,9 +443,6 @@
     for c in (1, 3):
         a_z[c] = raw("zl", far, c, 0)
     b_c = [ring.copy("core", pr_ref.at[1 - core, w], got_core.at[k]) for k, w in enumerate((xf, xu, xd, x))]
-    for one in loads:
-        one.wait()
-    load_r.wait()
 
     q2 = {}
 
@@ -493,9 +472,9 @@
 
     def pass_plain(c):
         if c < 2:
-            q_d[c] = ring.copy("y-", pc.at[DOWN, chunk(c)], got_c.at[5, chunk(c)])
+            q_d[c] = ring.copy("y-", pc_ref.at[wanted[DOWN], chunk(c)], got_c.at[5, chunk(c)])
         else:
-            q_u[c] = ring.copy("y+", pc.at[UP, chunk(c)], got_c.at[4, chunk(c)])
+            q_u[c] = ring.copy("y+", pc_ref.at[wanted[UP], chunk(c)], got_c.at[4, chunk(c)])
 
     pass_far(0)
     a_u[2], a_d[2] = raw("y+", up, 2, 1), raw("y-", down, 2, 2)
@@ -564,7 +543,7 @@
     def col_sum(start, size):
         at = pl.ds(start, size)
         return (
-            pc[MINE, at].astype(F32) + got_c[3, at].astype(F32)
+            pc_ref[wanted[MINE], at].astype(F32) + got_c[3, at].astype(F32)
             + got_c[4, at].astype(F32) + got_c[5, at].astype(F32)
         )
 
@@ -592,14 +571,12 @@
     return pl.pallas_call(
         reduce_kernel,
         out_shape=(
-            jax.ShapeDtypeStruct((DP, (FULL + 1) * L), F32),
-            jax.ShapeDtypeStruct((DP, L), F32),
+            pltpu.VMEM((DP, (FULL + 1) * L), F32),
+            pltpu.VMEM((DP, L), F32),
         ),
-        in_specs=[ANY, ANY],
+        in_specs=[IN_VMEM] * 2,
         out_specs=(IN_VMEM,) * 2,
         scratch_shapes=[
-            pltpu.VMEM((5, PACK, L), BF16),
-            pltpu.VMEM((4, 4, DP, L), F32),
             pltpu.VMEM((6, PACK, L), BF16),
             pltpu.VMEM((PACK, L), BF16),
             pltpu.VMEM((3, PACK, L), BF16),
@@ -613,10 +590,9 @@
             pltpu.VMEM((4, DP, L), F32),
             pltpu.SemaphoreType.DMA((COPIES,)),
             pltpu.SemaphoreType.DMA((COPIES,)),
-            pltpu.SemaphoreType.DMA((6,)),
         ],
         compiler_params=pltpu.CompilerParams(
-            collective_id=1, has_side_effects=True, vmem_limit_bytes=VMEM_LIMIT
+            collective_id=1, has_side_effects=True, vmem_limit_bytes=20 * MIB
         ),
         name="reduce",
     )(pc, pr)
@@ -640,14 +616,17 @@
         ),
         in_specs=[IN_VMEM] * 2,
         out_specs=(IN_VMEM,) * 4,
+        compiler_params=pltpu.CompilerParams(vmem_limit_bytes=8 * MIB),
         name="outputs",
     )(oc, orow)
 
 
 def body(row_vecs, row_bias, col_vecs, col_bias, row_block, col_block, counts, block_totals):
-    gc, gr, rn = gather(col_vecs.T, col_bias[None], row_vecs.T, row_bias[None])
+    gc, gr, rn, counts = gather(
+        col_vecs.T, col_bias, row_vecs.T, row_bias, counts.reshape(CAP, L, L)
+    )
     pc, pr = blocks(
-        block_totals, row_block, col_block, counts.reshape(CAP, L, L), gc,
+        block_totals, row_block, col_block, counts, gc,
         gr.reshape(ROW_TILES, DP, L), rn.reshape(ROW_TILES, L, DP),
     )
     grad_rows, grad_row_bias, grad_cols, grad_col_bias = outputs(*reduce(pc, pr.reshape(2, 4, 4, DP, L)))

time: 111 us -> 89.2 us (0.80)
  Pallas kernels: 109 us -> 88.4 us
  local copies, waits for them, and re-layouts: 1.26 us -> 0.01 us
    pallas_call x3, Pallas kernels: 107 us -> 87.3 us  [the longest x1 38 us: reduce(): pl.pallas_call(reduce_kernel, out_shape=(pltpu.VMEM((DP, (FULL + 1) * L),...]
    broadcast_in_dim x1 -> x0, local copies, waits for them, and re-layouts: 1.26 us -> none  [body(): gc, gr, rn = gather(col_vecs.T, col_bias[None], row_vecs.T, row_bias[None])]
    pallas_call x1, Pallas kernels: 2.34 us -> 1.11 us  [outputs(): pl.pallas_call(outputs_kernel, out_shape=(jax.ShapeDtypeStruct((D, L), F3...]
where the time goes in v3:
time: 89.2 us; the launch traced here: 89.1 us
  Pallas kernels  88.4 us (99%)
    pallas_call x1, Pallas kernels, reduce(): pl.pallas_call(reduce_kernel, out_shape=(pltpu.VMEM((DP, (FULL + 1) * L),...  38 us
    pallas_call x1, Pallas kernels, gather(): pl.pallas_call(gather_kernel, out_shape=(pltpu.VMEM((TILES, L), BF16), pl...  36.4 us
    pallas_call x1, Pallas kernels, blocks(): pl.pallas_call(blocks_kernel, out_shape=(pltpu.VMEM((SHARDS, PACK, L), BF...  12.9 us

profile of v3, /device:TPU:1, one launch (start us, length us, event | category | flops | bytes accessed | tf_op | source)
XLA Modules:
  0.0 89.1 jit_solution(2445065958758277556)
XLA Ops:
  0.6 0.0 copy-start
  0.6 0.0 copy-start.1
  0.7 0.0 copy-start.2
  0.7 36.4 %gather.1 = (bf16[17664,128]{1,0:T(8,128)(2,1)S(1)}, bf16[2,4,4,304,128]{4,3,2,1,0:T(8,128)(2,1)S(1)}, bf16[2,4,4,128,304]{4,3,2,1,0:T(8,128)(2,1)S(1)}, s32[128,128,128]{2,1,0:T(8,128)S(1)}) custom-call(bf16[300,800]{1,0:T(8,128)(2,1)} %bitcast.12, bf16[800]{0:T(1024)(128)(2,1)} %cb_hbm.1, bf16[300,128]{1,0:T(8,128)(2,1)} %bitcast.13, ...), custom_call_target="tpu_custom_call" | custom-call | tf_op jit(solution)/shard_map/gather/pallas_call | solution.py:269
  37.0 0.0 copy-done
  37.0 0.0 copy-done.1
  37.1 0.0 copy-done.2
  37.1 12.9 %blocks.1 = (bf16[8,1904,128]{2,1,0:T(8,128)(2,1)S(1)}, f32[32,304,128]{2,1,0:T(8,128)S(1)}) custom-call(s32[8,32]{1,0:T(8,128)S(1)} %copy-done, s32[1,1,128]{2,1,0:T(1,128)S(1)} %copy-done.1, s32[1,1,128]{2,1,0:T(1,128)S(1)} %copy-done.2, s32[128,128,128]{2,1,0:T(8,128)S(1)} %get-tuple-element.16.counts, bf16[17664,128]{1,0:T(8,128)(2,1)S(1)} %get-tuple-element.17.ct, ...), custom_call_target="tpu_custom_call" | custom-call | tf_op jit(solution)/shard_map/blocks/pallas_call | solution.py:397
  50.0 38.0 %reduce.1 = (f32[304,896]{1,0:T(8,128)S(1)}, f32[304,128]{1,0:T(8,128)S(1)}) custom-call(bf16[8,1904,128]{2,1,0:T(8,128)(2,1)S(1)} %get-tuple-element.20.pc_ref, f32[2,4,4,304,128]{4,3,2,1,0:T(8,128)S(1)} %bitcast.8), custom_call_target="tpu_custom_call" | custom-call | tf_op jit(solution)/shard_map/reduce/pallas_call | solution.py:571
  88.0 1.1 %outputs.1 = (f32[300,128]{1,0:T(8,128)}, f32[128]{0:T(128)}, f32[300,800]{1,0:T(8,128)}, f32[800]{0:T(1024)}) custom-call(f32[304,896]{1,0:T(8,128)S(1)} %get-tuple-element.22.oc_ref, f32[304,128]{1,0:T(8,128)S(1)} %get-tuple-element.23.or_ref), custom_call_target="tpu_custom_call" | custom-call | tf_op jit(solution)/shard_map/outputs/pallas_call | solution.py:609
Async XLA Ops:
  0.6 36.4 %copy-start = (s32[8,32]{1,0:T(8,128)S(1)}, s32[8,32]{1,0:T(8,128)}, u32[]{:S(2)}) copy-start(s32[8,32]{1,0:T(8,128)} %total_ref.1) | copy-start | bytes 3076
  0.6 36.4 %copy-start.1 = (s32[1,1,128]{2,1,0:T(1,128)S(1)}, s32[1,1,128]{2,1,0:T(1,128)}, u32[]{:S(2)}) copy-start(s32[1,1,128]{2,1,0:T(1,128)} %rid_ref.1) | copy-start | bytes 1540
  0.7 36.4 %copy-start.2 = (s32[1,1,128]{2,1,0:T(1,128)S(1)}, s32[1,1,128]{2,1,0:T(1,128)}, u32[]{:S(2)}) copy-start(s32[1,1,128]{2,1,0:T(1,128)} %cid_ref.1) | copy-start | bytes 1540

commit v4 on v3

--- a/solution.py
+++ b/solution.py
@@ -28,6 +28,7 @@
 CAP = 128
 TILES = SHARDS * PACK + 8 * DP
 GROUP = 16
+DEEP = 256
 MIB = 1024 * 1024
 
 
@@ -100,7 +101,7 @@
 COPIES = 48
 
 
-def gather_kernel(cv_hbm, cb_hbm, rv_hbm, rb_hbm, counts_hbm, gc, gr, rn, counts,
+def gather_kernel(cv_hbm, cb_hbm, rv_hbm, rb_hbm, counts_hbm, gc, gr, rn, counts, acc_c, acc_r,
                   cv_ref, cb_ref, rv_ref, rb_ref, wc, last, send, recv, local):
     pairs = ((rv_hbm, rv_ref), (rb_hbm, rb_ref), (cv_hbm, cv_ref), (cb_hbm, cb_ref), (counts_hbm, counts))
     loads = [pltpu.make_async_copy(src, dst, local.at[1 + k]) for k, (src, dst) in enumerate(pairs)]
@@ -244,6 +245,14 @@
     c_z[3].wait_recv()
     o_u[3], o_d[3] = pass_on("y+", other, 3), pass_on("y-", other, 3)
 
+    @pl.loop(0, COL_TILES)
+    def _(i):
+        acc_c[i] = jnp.zeros((DP, L), F32)
+
+    @pl.loop(0, ROW_TILES)
+    def _(i):
+        acc_r[i] = jnp.zeros((DP, L), F32)
+
     turn(core, x)
     for one in x_f.values():
         one.wait_recv()
@@ -254,13 +263,14 @@
         got.wait_recv()
         turn(1 - core, xx)
 
-    rest = [c_u[2], c_u[3], c_d[0], c_d[1]]
-    for c in range(4):
-        rest += [o_u[c], o_d[c], f_z[c]]
-    for got in rest:
+    for got in (c_u[2], c_u[3], c_d[0], c_d[1]):
         got.wait_recv()
     own_c.wait()
-    merge_tiles(gc)
+    merge_tiles(gc, zl)
+    for c in range(4):
+        for got in (o_u[c], o_d[c], f_z[c]):
+            got.wait_recv()
+    merge_tiles(gc, 1 - zl)
     ring.finish()
     loads[4].wait()
 
@@ -273,9 +283,11 @@
             pltpu.VMEM((2, 4, 4, DP, L), BF16),
             pltpu.VMEM((2, 4, 4, L, DP), BF16),
             pltpu.VMEM((CAP, L, L), jnp.int32),
+            pltpu.VMEM((COL_TILES, DP, L), F32),
+            pltpu.VMEM((ROW_TILES, DP, L), F32),
         ),
         in_specs=[IN_HBM] * 5,
-        out_specs=(IN_VMEM,) * 4,
+        out_specs=(IN_VMEM,) * 6,
         scratch_shapes=[
             pltpu.VMEM((D, SHARD), BF16),
             pltpu.VMEM((SHARD,), BF16),
@@ -294,26 +306,24 @@
     )(*(pltpu.with_memory_space_constraint(a, pltpu.HBM) for a in (cv, cb, rv, rb, counts)))
 
 
-def merge_tiles(ct):
+def merge_tiles(ct, quad):
     lane = lax.broadcasted_iota(jnp.int32, (DP, L), 1)
 
-    def first(s):
-        return ct[s * PACK : s * PACK + DP].astype(F32)
-
-    def tail(s):
-        part = ct[s * PACK + FULL * DP : (s + 1) * PACK].astype(F32)
-        turns = [(32 * (s % 4) - 32 * q) % L for q in range(4)]
-        return jnp.concatenate([pltpu.roll(part, n, 1) if n else part for n in turns], axis=0)[:DP]
-
-    for s in range(SHARDS):
-        k = s % 4
-        tile = tail(s)
+    def rows_at(n, size):
+        return pl.ds(pl.multiple_of(n, 16), size)
+
+    def first(k):
+        return ct[rows_at((quad * 4 + k) * PACK, DP)].astype(F32)
+
+    for k in range(4):
+        part = ct[rows_at((quad * 4 + k) * PACK + FULL * DP, QR)].astype(F32)
+        turns = [(32 * k - 32 * q) % L for q in range(4)]
+        tile = jnp.concatenate([pltpu.roll(part, n, 1) if n else part for n in turns], axis=0)[:DP]
         if k:
-            tile = jnp.where(lane < 32 * k, first(s), tile)
+            tile = jnp.where(lane < 32 * k, first(k), tile)
         if k < 3:
-            tile = jnp.where(lane < 32 * (k + 1), tile, first(s + 1))
-        at = SHARDS * PACK + s * DP
-        ct[at : at + DP] = tile.astype(BF16)
+            tile = jnp.where(lane < 32 * (k + 1), tile, first(k + 1))
+        ct[rows_at(SHARDS * PACK + (quad * 4 + k) * DP, DP)] = tile.astype(BF16)
 
 
 def tile_at(b):
@@ -347,18 +357,10 @@
 LN2 = 0.6931471805599453
 
 
-def blocks_kernel(total_ref, rid_ref, cid_ref, counts, ct, rt, rn, pc, acc_r, acc_c):
+def blocks_kernel(total_ref, rid_ref, cid_ref, counts, ct, rt, rn, zero_c, zero_r, pc, acc_r, acc_c):
     row, col = lax.axis_index("row"), lax.axis_index("col")
     total = total_ref[row, col]
     groups = (total + GROUP - 1) // GROUP
-
-    @pl.loop(0, COL_TILES)
-    def _(i):
-        acc_c[i] = jnp.zeros((DP, L), F32)
-
-    @pl.loop(0, ROW_TILES)
-    def _(i):
-        acc_r[i] = jnp.zeros((DP, L), F32)
 
     @pl.loop(0, groups)
     def _(g):
@@ -369,9 +371,10 @@
             rid = rid % 2 * 16 + rid // 2 % 4 * 4 + rid // 8
             rids.append(rid)
             cids.append(cid)
-            tile = pl.ds(pl.multiple_of(tile_at(cid), 16), DP)
-            tiles.append(tile)
-            scores = jnp.dot(rn[rid], ct[tile], preferred_element_type=F32)
+            at = pl.multiple_of(tile_at(cid), 16)
+            tiles.append(pl.ds(at, DP))
+            scores = jnp.dot(rn[rid, :, :DEEP], ct[pl.ds(at, DEEP)], preferred_element_type=F32)
+            scores += jnp.dot(rn[rid, :, DEEP:], ct[pl.ds(at + DEEP, DP - DEEP)], preferred_element_type=F32)
             x = counts[n]
             least = jnp.where(n < total, 0, jnp.int32(2**31 - 1))
             log2x = jnp.log2(jnp.maximum(x.astype(F32), 1.0))
@@ -393,19 +396,20 @@
             pc[s, at : at + part.shape[0]] = part.astype(BF16)
 
 
-def blocks(totals, rid, cid, counts, gc, gr, rn):
+def blocks(totals, rid, cid, counts, gc, gr, rn, acc_c, acc_r):
     return pl.pallas_call(
         blocks_kernel,
         out_shape=(
             pltpu.VMEM((SHARDS, PACK, L), BF16),
             pltpu.VMEM((ROW_TILES, DP, L), F32),
+            pltpu.VMEM((COL_TILES, DP, L), F32),
         ),
-        in_specs=[IN_SMEM] * 3 + [IN_VMEM] * 4,
-        out_specs=(IN_VMEM, IN_VMEM),
-        scratch_shapes=[pltpu.VMEM((COL_TILES, DP, L), F32)],
-        compiler_params=pltpu.CompilerParams(vmem_limit_bytes=14 * MIB),
+        in_specs=[IN_SMEM] * 3 + [IN_VMEM] * 6,
+        out_specs=(IN_VMEM,) * 3,
+        input_output_aliases={7: 2, 8: 1},
+        compiler_params=pltpu.CompilerParams(vmem_limit_bytes=8 * MIB),
         name="blocks",
-    )(totals, rid, cid, counts, gc, gr, rn)
+    )(totals, rid, cid, counts, gc, gr, rn, acc_c, acc_r)
 
 
 def reduce_kernel(pc_ref, pr_ref, oc_ref, or_ref,
@@ -476,65 +480,77 @@
         else:
             q_u[c] = ring.copy("y+", pc_ref.at[wanted[UP], chunk(c)], got_c.at[4, chunk(c)])
 
+    x_far, x_up, x_down = {}, {}, {}
+
+    def row_far():
+        b_c[0].wait_recv()
+        for k, z in enumerate((zf, zu, zd, zh)):
+            put_x[0, z] = (pr[xf, z] + got_core[0, z]).astype(BF16)
+            x_far[k] = ring.copy("x-" if k % 2 else "x+", put_x.at[0, z], half_x.at[z])
+
+    def row_near(to, k):
+        z = (zf, zu, zd, zh)[k]
+        up_side = to == "x+"
+        one = pr[xu, z] + got_core[1, z] if up_side else pr[xd, z] + got_core[2, z]
+        if up_side == (k % 2 == 0):
+            x_far[k].wait_recv()
+            one = one + half_x[z].astype(F32)
+        slot, side = (1, 0) if up_side else (2, 1)
+        put_x[slot, z] = one.astype(BF16)
+        (x_up if up_side else x_down)[k] = ring.copy(to, put_x.at[slot, z], got_x.at[side, z])
+
+    def row_sum(k):
+        z = (zf, zu, zd, zh)[k]
+        x_up[k].wait_recv()
+        x_down[k].wait_recv()
+        return pr[x, z] + got_core[3, z] + got_x[0, z].astype(F32) + got_x[1, z].astype(F32)
+
     pass_far(0)
     a_u[2], a_d[2] = raw("y+", up, 2, 1), raw("y-", down, 2, 2)
-    b_c[0].wait_recv()
-    for z in range(4):
-        put_x[0, z] = (pr[xf, z] + got_core[0, z]).astype(BF16)
-    b_x0 = ring.copy("x+", put_x.at[0, pl.ds(0, 2)], half_x.at[0])
-    b_x1 = ring.copy("x-", put_x.at[0, pl.ds(2, 2)], half_x.at[1])
+    row_far()
     pass_far(2)
     a_u[3], a_d[3] = raw("y+", up, 3, 1), raw("y-", down, 3, 2)
+    b_c[1].wait_recv()
+    b_c[2].wait_recv()
+    row_near("x-", 0)
+    row_near("x+", 1)
     pass_other(0)
     pass_far(1)
+    row_near("x+", 0)
+    row_near("x-", 1)
+    row_near("x-", 2)
+    row_near("x+", 3)
     pass_other(1)
-
-    b_c[1].wait_recv()
-    b_x0.wait_recv()
-    for z in range(4):
-        one = pr[xu, z] + got_core[1, z]
-        if z < 2:
-            one = one + half_x[0, z].astype(F32)
-        put_x[1, z] = one.astype(BF16)
-    b_x2 = ring.copy("x+", put_x.at[1], got_x.at[0])
-    b_c[2].wait_recv()
-    b_x1.wait_recv()
-    for z in range(4):
-        one = pr[xd, z] + got_core[2, z]
-        if z >= 2:
-            one = one + half_x[1, z - 2].astype(F32)
-        put_x[2, z] = one.astype(BF16)
-    b_x3 = ring.copy("x-", put_x.at[2], got_x.at[1])
-
     pass_far(3)
     pass_plain(0)
     pass_plain(2)
+    row_near("x+", 2)
+    row_near("x-", 3)
     pass_near(0)
     pass_near(2)
+
+    b_c[3].wait_recv()
+    rlo, rhi = pl.ds(0, RHALF), pl.ds(RHALF, DP - RHALF)
+    put_z[0] = row_sum(0).astype(BF16)
+    b_z0 = ring.copy("zh+", put_z.at[0, rlo], half_z.at[rlo])
+    b_z1 = ring.copy("zh-", put_z.at[0, rhi], half_z.at[rhi])
     pass_other(2)
     pass_plain(1)
     pass_plain(3)
+    u[0] = row_sum(1)
+    u[1] = row_sum(2)
     pass_near(1)
     pass_near(3)
-    pass_other(3)
-
-    b_c[3].wait_recv()
-    b_x2.wait_recv()
-    b_x3.wait_recv()
-    for z in range(4):
-        u[z] = pr[x, z] + got_core[3, z] + got_x[0, z].astype(F32) + got_x[1, z].astype(F32)
-    put_z[0] = u[zf].astype(BF16)
-    rlo, rhi = pl.ds(0, RHALF), pl.ds(RHALF, DP - RHALF)
-    b_z0 = ring.copy("zh+", put_z.at[0, rlo], half_z.at[rlo])
-    b_z1 = ring.copy("zh-", put_z.at[0, rhi], half_z.at[rhi])
     b_z0.wait_recv()
-    put_z[1, 0:RHALF] = (u[zu, 0:RHALF] + half_z[0:RHALF].astype(F32)).astype(BF16)
-    put_z[1, RHALF:DP] = u[zu, RHALF:DP].astype(BF16)
+    put_z[1, 0:RHALF] = (u[0, 0:RHALF] + half_z[0:RHALF].astype(F32)).astype(BF16)
+    put_z[1, RHALF:DP] = u[0, RHALF:DP].astype(BF16)
     b_z2 = ring.copy("zh+", put_z.at[1], got_z.at[0])
     b_z1.wait_recv()
-    put_z[2, 0:RHALF] = u[zd, 0:RHALF].astype(BF16)
-    put_z[2, RHALF:DP] = (u[zd, RHALF:DP] + half_z[RHALF:DP].astype(F32)).astype(BF16)
+    put_z[2, 0:RHALF] = u[1, 0:RHALF].astype(BF16)
+    put_z[2, RHALF:DP] = (u[1, RHALF:DP] + half_z[RHALF:DP].astype(F32)).astype(BF16)
     b_z3 = ring.copy("zh-", put_z.at[2], got_z.at[1])
+    pass_other(3)
+    u[0] = row_sum(3)
 
     for c in range(4):
         for got in (qz, q_u, q_d):
@@ -563,7 +579,7 @@
 
     b_z2.wait_recv()
     b_z3.wait_recv()
-    or_ref[...] = u[zh] + got_z[0].astype(F32) + got_z[1].astype(F32)
+    or_ref[...] = u[0] + got_z[0].astype(F32) + got_z[1].astype(F32)
     ring.finish()
 
 
@@ -583,11 +599,11 @@
             pltpu.VMEM((4, 4, DP, L), F32),
             pltpu.VMEM((2, 4, DP, L), BF16),
             pltpu.VMEM((3, 4, DP, L), BF16),
-            pltpu.VMEM((2, 2, DP, L), BF16),
+            pltpu.VMEM((4, DP, L), BF16),
             pltpu.VMEM((DP, L), BF16),
             pltpu.VMEM((2, DP, L), BF16),
             pltpu.VMEM((3, DP, L), BF16),
-            pltpu.VMEM((4, DP, L), F32),
+            pltpu.VMEM((2, DP, L), F32),
             pltpu.SemaphoreType.DMA((COPIES,)),
             pltpu.SemaphoreType.DMA((COPIES,)),
         ],
@@ -622,12 +638,12 @@
 
 
 def body(row_vecs, row_bias, col_vecs, col_bias, row_block, col_block, counts, block_totals):
-    gc, gr, rn, counts = gather(
+    gc, gr, rn, counts, acc_c, acc_r = gather(
         col_vecs.T, col_bias, row_vecs.T, row_bias, counts.reshape(CAP, L, L)
     )
-    pc, pr = blocks(
+    pc, pr, _ = blocks(
         block_totals, row_block, col_block, counts, gc,
-        gr.reshape(ROW_TILES, DP, L), rn.reshape(ROW_TILES, L, DP),
+        gr.reshape(ROW_TILES, DP, L), rn.reshape(ROW_TILES, L, DP), acc_c, acc_r,
     )
     grad_rows, grad_row_bias, grad_cols, grad_col_bias = outputs(*reduce(pc, pr.reshape(2, 4, 4, DP, L)))
     return grad_rows.T, grad_row_bias, grad_cols.T, grad_col_bias

time: 89.2 us -> 84.2 us (0.944)
  Pallas kernels: 88.4 us -> 83.4 us
    pallas_call x1, Pallas kernels: 12.9 us -> 7.66 us  [blocks(): pl.pallas_call(blocks_kernel, out_shape=(pltpu.VMEM((SHARDS, PACK, L), BF...]
where the time goes in v4:
time: 84.2 us; the launch traced here: 84.1 us
  Pallas kernels  83.4 us (99%)
    pallas_call x1, Pallas kernels, reduce(): pl.pallas_call(reduce_kernel, out_shape=(pltpu.VMEM((DP, (FULL + 1) * L),...  38.1 us
    pallas_call x1, Pallas kernels, gather(): pl.pallas_call(gather_kernel, out_shape=(pltpu.VMEM((TILES, L), BF16), pl...  36.5 us
    pallas_call x1, Pallas kernels, blocks(): pl.pallas_call(blocks_kernel, out_shape=(pltpu.VMEM((SHARDS, PACK, L), BF...  7.66 us

profile of v4, /device:TPU:1, one launch (start us, length us, event | category | flops | bytes accessed | tf_op | source)
XLA Modules:
  0.0 84.1 jit_solution(9802507995309022050)
XLA Ops:
  0.6 0.0 copy-start
  0.6 0.0 copy-start.2
  0.7 0.0 copy-start.1
  0.7 36.5 %gather.1 = (bf16[17664,128]{1,0:T(8,128)(2,1)S(1)}, bf16[2,4,4,304,128]{4,3,2,1,0:T(8,128)(2,1)S(1)}, bf16[2,4,4,128,304]{4,3,2,1,0:T(8,128)(2,1)S(1)}, s32[128...) custom-call(bf16[300,800]{1,0:T(8,128)(2,1)} %bitcast.12, bf16[800]{0:T(1024)(128)(2,1)} %cb_hbm.1, ...), custom_call_target="tpu_custom_call" | custom-call | tf_op jit(solution)/shard_map/gather/pallas_call | solution.py:279
  37.2 0.0 copy-done
  37.2 0.0 copy-done.2
  37.2 0.0 copy-done.1
  37.2 7.7 %blocks.1 = (bf16[8,1904,128]{2,1,0:T(8,128)(2,1)S(1)}, f32[32,304,128]{2,1,0:T(8,128)S(1)}, f32[50,304,128]{2,1,0:T(8,128)S(1)}) custom-call(s32[8,32]{1,0:T(8,128)S(1)} %copy-done, s32[1,1,128]{2,1,0:T(1,128)S(1)} %copy-done.1, s32[1,1,128]{2,1,0:T(1,128)S(1)} %copy-done.2, ...), custom_call_target="tpu_custom_call", output_to_operand_aliasing={{2}: (7, {}), {1}: (8, {})} | custom-call | tf_op jit(solution)/shard_map/blocks/pallas_call | solution.py:400
  44.9 38.1 %reduce.1 = (f32[304,896]{1,0:T(8,128)S(1)}, f32[304,128]{1,0:T(8,128)S(1)}) custom-call(bf16[8,1904,128]{2,1,0:T(8,128)(2,1)S(1)} %get-tuple-element.24.pc_ref, f32[2,4,4,304,128]{4,3,2,1,0:T(8,128)S(1)} %bitcast.8), custom_call_target="tpu_custom_call" | custom-call | tf_op jit(solution)/shard_map/reduce/pallas_call | solution.py:587
  83.0 1.1 %outputs.1 = (f32[300,128]{1,0:T(8,128)}, f32[128]{0:T(128)}, f32[300,800]{1,0:T(8,128)}, f32[800]{0:T(1024)}) custom-call(f32[304,896]{1,0:T(8,128)S(1)} %get-tuple-element.26.oc_ref, f32[304,128]{1,0:T(8,128)S(1)} %get-tuple-element.27.or_ref), custom_call_target="tpu_custom_call" | custom-call | tf_op jit(solution)/shard_map/outputs/pallas_call | solution.py:625
Async XLA Ops:
  0.6 36.6 %copy-start = (s32[8,32]{1,0:T(8,128)S(1)}, s32[8,32]{1,0:T(8,128)}, u32[]{:S(2)}) copy-start(s32[8,32]{1,0:T(8,128)} %total_ref.1) | copy-start | bytes 3076
  0.6 36.6 %copy-start.2 = (s32[1,1,128]{2,1,0:T(1,128)S(1)}, s32[1,1,128]{2,1,0:T(1,128)}, u32[]{:S(2)}) copy-start(s32[1,1,128]{2,1,0:T(1,128)} %cid_ref.1) | copy-start | bytes 1540
  0.7 36.6 %copy-start.1 = (s32[1,1,128]{2,1,0:T(1,128)S(1)}, s32[1,1,128]{2,1,0:T(1,128)}, u32[]{:S(2)}) copy-start(s32[1,1,128]{2,1,0:T(1,128)} %rid_ref.1) | copy-start | bytes 1540

commit v5 on v4

--- a/solution.py
+++ b/solution.py
@@ -27,7 +27,8 @@
 QUAD = COL_TILES // 2
 CAP = 128
 TILES = SHARDS * PACK + 8 * DP
-GROUP = 16
+GROUP = 32
+BEHIND = 4
 DEEP = 256
 MIB = 1024 * 1024
 
@@ -327,52 +328,48 @@
 
 
 def tile_at(b):
-    quad, j = b // QUAD, b % QUAD
-    k, t = j // FULL, j % FULL
+    quad = (b >= QUAD).astype(jnp.int32)
+    j = b - QUAD * quad
+    k = (j * 43) >> 8
+    t = j - FULL * k
     shared = (k > 0) & (t == 0)
-    return jnp.where(shared, SHARDS * PACK + (quad * 4 + k - 1) * DP, (quad * 4 + k) * PACK + t * DP)
-
-
-def pack_shard(tiles, s):
-    k = s % 4
-    base = (SHARD * s) // L
+    at = jnp.where(shared, SHARDS * PACK + (quad * 4 + k - 1) * DP, (quad * 4 + k) * PACK + t * DP)
+    return pl.multiple_of(at, 16)
+
+
+def pack_shard(tiles, y, zl, packed, slot):
+    base, shift = QUAD * zl + FULL * y, 32 * y
     lane = lax.broadcasted_iota(jnp.int32, (DP, L), 1)
     lane_q = lax.broadcasted_iota(jnp.int32, (QR, L), 1)
     after = tiles[base + FULL]
-    head = tiles[base]
-    if k:
-        head = jnp.where(lane < 32 * k, after, head)
-    parts = [(0, head)] + [(t * DP, tiles[base + t]) for t in range(1, FULL)]
+    packed[slot, 0:DP] = jnp.where(lane < shift, after, tiles[base]).astype(BF16)
+    for t in range(1, FULL):
+        packed[slot, t * DP : (t + 1) * DP] = tiles[base + t].astype(BF16)
     after = jnp.concatenate([after, jnp.zeros((4 * QR - DP, L), F32)], axis=0)
     tail = None
     for q in range(4):
-        n = (32 * q - 32 * k) % L
-        part = after[q * QR : (q + 1) * QR]
-        part = pltpu.roll(part, n, 1) if n else part
+        part = pltpu.roll(after[q * QR : (q + 1) * QR], (32 * q + L - shift) % L, 1)
         tail = part if q == 0 else jnp.where(lane_q < 32 * q, tail, part)
-    return parts + [(FULL * DP, tail)]
+    packed[slot, FULL * DP : PACK] = tail.astype(BF16)
 
 
 LOG2_100 = 6.643856189774724
 LN2 = 0.6931471805599453
 
 
-def blocks_kernel(total_ref, rid_ref, cid_ref, counts, ct, rt, rn, zero_c, zero_r, pc, acc_r, acc_c):
+def blocks_kernel(total_ref, rid_ref, cid_ref, counts, ct, rt, rn, zero_c, zero_r, acc_c, acc_r):
     row, col = lax.axis_index("row"), lax.axis_index("col")
     total = total_ref[row, col]
     groups = (total + GROUP - 1) // GROUP
 
     @pl.loop(0, groups)
     def _(g):
-        terms, rids, cids, tiles = [], [], [], []
-        for k in range(GROUP):
-            n = g * GROUP + k
+        slots = []
+
+        def terms_of(n):
             rid, cid = rid_ref[0, 0, n], cid_ref[0, 0, n]
-            rid = rid % 2 * 16 + rid // 2 % 4 * 4 + rid // 8
-            rids.append(rid)
-            cids.append(cid)
-            at = pl.multiple_of(tile_at(cid), 16)
-            tiles.append(pl.ds(at, DP))
+            rid = ((rid & 1) << 4) + (((rid >> 1) & 3) << 2) + (rid >> 3)
+            at = tile_at(cid)
             scores = jnp.dot(rn[rid, :, :DEEP], ct[pl.ds(at, DEEP)], preferred_element_type=F32)
             scores += jnp.dot(rn[rid, :, DEEP:], ct[pl.ds(at + DEEP, DP - DEEP)], preferred_element_type=F32)
             x = counts[n]
@@ -380,40 +377,42 @@
             log2x = jnp.log2(jnp.maximum(x.astype(F32), 1.0))
             weight2 = jnp.exp2(jnp.minimum(0.75 * log2x + (1.0 - 0.75 * LOG2_100), 1.0))
             term = weight2 * (scores - LN2 * log2x)
-            terms.append(jnp.where(x > least, term, 0.0).astype(BF16))
-        for k in range(GROUP):
-            term, none = terms[k], jnp.zeros((L, L), BF16)
+            return rid, cid, at, jnp.where(x > least, term, 0.0).astype(BF16)
+
+        def add(rid, cid, at, term):
+            none = jnp.zeros((L, L), BF16)
             both = jnp.concatenate(
                 [jnp.concatenate([term, none], axis=1), jnp.concatenate([none, term.T], axis=1)], axis=0
             )
-            vecs = jnp.concatenate([rt[rids[k]], ct[tiles[k]]], axis=1)
+            vecs = jnp.concatenate([rt[rid], ct[pl.ds(at, DP)]], axis=1)
             grads = jnp.dot(vecs, both, preferred_element_type=F32)
-            acc_c[cids[k]] += grads[:, :L]
-            acc_r[rids[k]] += grads[:, L:]
-
-    for s in range(SHARDS):
-        for at, part in pack_shard(acc_c, s):
-            pc[s, at : at + part.shape[0]] = part.astype(BF16)
+            acc_c[cid] += grads[:, :L]
+            acc_r[rid] += grads[:, L:]
+
+        for k in range(GROUP + BEHIND):
+            if k < GROUP:
+                slots.append(terms_of(g * GROUP + k))
+            if k >= BEHIND:
+                add(*slots[k - BEHIND])
 
 
 def blocks(totals, rid, cid, counts, gc, gr, rn, acc_c, acc_r):
     return pl.pallas_call(
         blocks_kernel,
         out_shape=(
-            pltpu.VMEM((SHARDS, PACK, L), BF16),
+            pltpu.VMEM((COL_TILES, DP, L), F32),
             pltpu.VMEM((ROW_TILES, DP, L), F32),
-            pltpu.VMEM((COL_TILES, DP, L), F32),
         ),
         in_specs=[IN_SMEM] * 3 + [IN_VMEM] * 6,
-        out_specs=(IN_VMEM,) * 3,
-        input_output_aliases={7: 2, 8: 1},
+        out_specs=(IN_VMEM,) * 2,
+        input_output_aliases={7: 0, 8: 1},
         compiler_params=pltpu.CompilerParams(vmem_limit_bytes=8 * MIB),
         name="blocks",
     )(totals, rid, cid, counts, gc, gr, rn, acc_c, acc_r)
 
 
-def reduce_kernel(pc_ref, pr_ref, oc_ref, or_ref,
-                  got_c, half_c, put_c, got_core, got_x, put_x, half_x, half_z, got_z, put_z, u,
+def reduce_kernel(acc_ref, pr_ref, oc_ref, or_ref,
+                  pc, fin, got_c, half_c, put_c, got_core, got_x, put_x, half_x, half_z, got_z, put_z, u,
                   send, recv):
     ring = Ring(send, recv)
     y, zl, core, x, zh = ring.y, ring.zl, ring.core, ring.x, ring.zh
@@ -422,30 +421,36 @@
     up, down, far = (y + 1) % 4, (y + 3) % 4, (y + 2) % 4
     xu, xd, xf = (x + 1) % 4, (x + 3) % 4, (x + 2) % 4
     zu, zd, zf = (zh + 1) % 4, (zh + 3) % 4, (zh + 2) % 4
-    FAR, OTHER, UP, DOWN, MINE = range(5)
-    wanted = (row_of(far, zl), row_of(y, zo), row_of(up, zl), row_of(down, zl), row_of(y, zl))
+    FAR_O, UP_O, DOWN_O, FAR, OTHER, UP, DOWN, MINE = range(SHARDS)
+    wanted = ((far, zo), (up, zo), (down, zo), (far, zl), (y, zo), (up, zl), (down, zl), (y, zl))
+
+    def pack(*slots):
+        for k in slots:
+            pack_shard(acc_ref, *wanted[k], pc, k)
+
+    pack(FAR_O, UP_O, DOWN_O)
     pr = pr_ref.at[core]
     ring.meet(barrier)
 
-    def raw(to, y_to, c, k):
-        return ring.copy(to, pc_ref.at[row_of(y_to, zo), chunk(c)], got_c.at[k, chunk(c)])
+    def raw(to, k, c, got):
+        return ring.copy(to, pc.at[k, chunk(c)], got_c.at[got, chunk(c)])
 
     def put(to, k, c, dst):
         return ring.copy(to, put_c.at[k, chunk(c)], dst.at[chunk(c)])
 
     def total(k, c, *more):
         at = chunk(c)
-        out = pc_ref[wanted[k], at].astype(F32)
+        out = pc[k, at].astype(F32)
         for one in more:
             out = out + one[at].astype(F32)
         return out
 
     a_z, a_u, a_d = {}, {}, {}
     for c in (0, 1):
-        a_z[2 * c] = raw("zl", far, 2 * c, 0)
-        a_u[c], a_d[c] = raw("y+", up, c, 1), raw("y-", down, c, 2)
+        a_z[2 * c] = raw("zl", FAR_O, 2 * c, 0)
+        a_u[c], a_d[c] = raw("y+", UP_O, c, 1), raw("y-", DOWN_O, c, 2)
     for c in (1, 3):
-        a_z[c] = raw("zl", far, c, 0)
+        a_z[c] = raw("zl", FAR_O, c, 0)
     b_c = [ring.copy("core", pr_ref.at[1 - core, w], got_core.at[k]) for k, w in enumerate((xf, xu, xd, x))]
 
     q2 = {}
@@ -476,9 +481,9 @@
 
     def pass_plain(c):
         if c < 2:
-            q_d[c] = ring.copy("y-", pc_ref.at[wanted[DOWN], chunk(c)], got_c.at[5, chunk(c)])
+            q_d[c] = ring.copy("y-", pc.at[DOWN, chunk(c)], got_c.at[5, chunk(c)])
         else:
-            q_u[c] = ring.copy("y+", pc_ref.at[wanted[UP], chunk(c)], got_c.at[4, chunk(c)])
+            q_u[c] = ring.copy("y+", pc.at[UP, chunk(c)], got_c.at[4, chunk(c)])
 
     x_far, x_up, x_down = {}, {}, {}
 
@@ -505,15 +510,17 @@
         x_down[k].wait_recv()
         return pr[x, z] + got_core[3, z] + got_x[0, z].astype(F32) + got_x[1, z].astype(F32)
 
+    pack(FAR)
     pass_far(0)
-    a_u[2], a_d[2] = raw("y+", up, 2, 1), raw("y-", down, 2, 2)
+    a_u[2], a_d[2] = raw("y+", UP_O, 2, 1), raw("y-", DOWN_O, 2, 2)
     row_far()
     pass_far(2)
-    a_u[3], a_d[3] = raw("y+", up, 3, 1), raw("y-", down, 3, 2)
+    a_u[3], a_d[3] = raw("y+", UP_O, 3, 1), raw("y-", DOWN_O, 3, 2)
     b_c[1].wait_recv()
     b_c[2].wait_recv()
     row_near("x-", 0)
     row_near("x+", 1)
+    pack(OTHER)
     pass_other(0)
     pass_far(1)
     row_near("x+", 0)
@@ -522,6 +529,7 @@
     row_near("x+", 3)
     pass_other(1)
     pass_far(3)
+    pack(UP, DOWN)
     pass_plain(0)
     pass_plain(2)
     row_near("x+", 2)
@@ -551,27 +559,22 @@
     b_z3 = ring.copy("zh-", put_z.at[2], got_z.at[1])
     pass_other(3)
     u[0] = row_sum(3)
+    pack(MINE)
 
     for c in range(4):
         for got in (qz, q_u, q_d):
             got[c].wait_recv()
-
-    def col_sum(start, size):
-        at = pl.ds(start, size)
-        return (
-            pc_ref[wanted[MINE], at].astype(F32) + got_c[3, at].astype(F32)
-            + got_c[4, at].astype(F32) + got_c[5, at].astype(F32)
-        )
+        fin[chunk(c)] = total(MINE, c, got_c.at[3], got_c.at[4], got_c.at[5])
 
     shift = 32 * y
     back = (L - shift) % L
     lane = lax.broadcasted_iota(jnp.int32, (DP, L), 1)
-    sums = [col_sum(t * DP, DP) for t in range(FULL)]
+    sums = [fin[t * DP : (t + 1) * DP] for t in range(FULL)]
     for t in range(FULL):
         oc_ref[:, t * L : (t + 1) * L] = pltpu.roll(
             jnp.where(lane < shift, sums[(t + 1) % FULL], sums[t]), back, 1
         )
-    tail = col_sum(FULL * DP, QR)
+    tail = fin[FULL * DP : PACK]
     for q in range(4):
         part = pltpu.roll(tail, L - 32 * q, 1) if q else tail
         rows = min(QR, DP - q * QR)
@@ -583,7 +586,7 @@
     ring.finish()
 
 
-def reduce(pc, pr):
+def reduce(acc_c, pr):
     return pl.pallas_call(
         reduce_kernel,
         out_shape=(
@@ -593,6 +596,8 @@
         in_specs=[IN_VMEM] * 2,
         out_specs=(IN_VMEM,) * 2,
         scratch_shapes=[
+            pltpu.VMEM((SHARDS, PACK, L), BF16),
+            pltpu.VMEM((PACK, L), F32),
             pltpu.VMEM((6, PACK, L), BF16),
             pltpu.VMEM((PACK, L), BF16),
             pltpu.VMEM((3, PACK, L), BF16),
@@ -611,7 +616,7 @@
             collective_id=1, has_side_effects=True, vmem_limit_bytes=20 * MIB
         ),
         name="reduce",
-    )(pc, pr)
+    )(acc_c, pr)
 
 
 def outputs_kernel(oc_ref, or_ref, row_ref, row_bias_ref, col_ref, col_bias_ref):
@@ -641,11 +646,11 @@
     gc, gr, rn, counts, acc_c, acc_r = gather(
         col_vecs.T, col_bias, row_vecs.T, row_bias, counts.reshape(CAP, L, L)
     )
-    pc, pr, _ = blocks(
+    acc_c, acc_r = blocks(
         block_totals, row_block, col_block, counts, gc,
         gr.reshape(ROW_TILES, DP, L), rn.reshape(ROW_TILES, L, DP), acc_c, acc_r,
     )
-    grad_rows, grad_row_bias, grad_cols, grad_col_bias = outputs(*reduce(pc, pr.reshape(2, 4, 4, DP, L)))
+    grad_rows, grad_row_bias, grad_cols, grad_col_bias = outputs(*reduce(acc_c, acc_r.reshape(2, 4, 4, DP, L)))
     return grad_rows.T, grad_row_bias, grad_cols.T, grad_col_bias
 
 

time: 84.2 us -> 82.1 us (0.975)
  Pallas kernels: 83.4 us -> 81.1 us
    pallas_call x1, Pallas kernels: 7.66 us -> 6.15 us  [blocks(): pl.pallas_call(blocks_kernel, out_shape=(pltpu.VMEM((COL_TILES, DP, L), F...]
where the time goes in v5:
time: 82.1 us; the launch traced here: 81.8 us
  Pallas kernels  81.1 us (99%)
    pallas_call x1, Pallas kernels, reduce(): pl.pallas_call(reduce_kernel, out_shape=(pltpu.VMEM((DP, (FULL + 1) * L),...  37.3 us
    pallas_call x1, Pallas kernels, gather(): pl.pallas_call(gather_kernel, out_shape=(pltpu.VMEM((TILES, L), BF16), pl...  36.5 us
    pallas_call x1, Pallas kernels, blocks(): pl.pallas_call(blocks_kernel, out_shape=(pltpu.VMEM((COL_TILES, DP, L), F...  6.15 us

profile of v5, /device:TPU:1, one launch (start us, length us, event | category | flops | bytes accessed | tf_op | source)
XLA Modules:
  0.0 81.8 jit_solution(2425690034879805610)
XLA Ops:
  0.6 0.0 copy-start
  0.6 0.0 copy-start.2
  0.7 0.0 copy-start.1
  0.7 36.5 %gather.1 = (bf16[17664,128]{1,0:T(8,128)(2,1)S(1)}, bf16[2,4,4,304,128]{4,3,2,1,0:T(8,128)(2,1)S(1)}, bf16[2,4,4,128,304]{4,3,2,1,0:T(8,128)(2,1)S(1)}, s32[128...) custom-call(bf16[300,800]{1,0:T(8,128)(2,1)} %bitcast.12, bf16[800]{0:T(1024)(128)(2,1)} %cb_hbm.1, ...), custom_call_target="tpu_custom_call" | custom-call | tf_op jit(solution)/shard_map/gather/pallas_call | solution.py:280
  37.2 0.0 copy-done
  37.2 0.0 copy-done.2
  37.2 0.0 copy-done.1
  37.2 6.1 %blocks.1 = (f32[50,304,128]{2,1,0:T(8,128)S(1)}, f32[32,304,128]{2,1,0:T(8,128)S(1)}) custom-call(s32[8,32]{1,0:T(8,128)S(1)} %copy-done, s32[1,1,128]{2,1,0:T(1,128)S(1)} %copy-done.1, s32[1,1,128]{2,1,0:T(1,128)S(1)} %copy-done.2, s32[128,128,128]{2,1,0:T(8,128)S(1)} %get-tuple-element.18.counts, ...), custom_call_target="tpu_custom_call", output_to_operand_aliasing={{0}: (7, {}), {1}: (8, {})} | custom-call | tf_op jit(solution)/shard_map/blocks/pallas_call | solution.py:400
  43.4 37.3 %reduce.1 = (f32[304,896]{1,0:T(8,128)S(1)}, f32[304,128]{1,0:T(8,128)S(1)}) custom-call(f32[50,304,128]{2,1,0:T(8,128)S(1)} %get-tuple-element.24.acc_ref, f32[2,4,4,304,128]{4,3,2,1,0:T(8,128)S(1)} %bitcast.8), custom_call_target="tpu_custom_call" | custom-call | tf_op jit(solution)/shard_map/reduce/pallas_call | solution.py:590
  80.7 1.1 %outputs.1 = (f32[300,128]{1,0:T(8,128)}, f32[128]{0:T(128)}, f32[300,800]{1,0:T(8,128)}, f32[800]{0:T(1024)}) custom-call(f32[304,896]{1,0:T(8,128)S(1)} %get-tuple-element.26.oc_ref, f32[304,128]{1,0:T(8,128)S(1)} %get-tuple-element.27.or_ref), custom_call_target="tpu_custom_call" | custom-call | tf_op jit(solution)/shard_map/outputs/pallas_call | solution.py:630
Async XLA Ops:
  0.6 36.6 %copy-start = (s32[8,32]{1,0:T(8,128)S(1)}, s32[8,32]{1,0:T(8,128)}, u32[]{:S(2)}) copy-start(s32[8,32]{1,0:T(8,128)} %total_ref.1) | copy-start | bytes 3076
  0.6 36.6 %copy-start.2 = (s32[1,1,128]{2,1,0:T(1,128)S(1)}, s32[1,1,128]{2,1,0:T(1,128)}, u32[]{:S(2)}) copy-start(s32[1,1,128]{2,1,0:T(1,128)} %cid_ref.1) | copy-start | bytes 1540
  0.7 36.6 %copy-start.1 = (s32[1,1,128]{2,1,0:T(1,128)S(1)}, s32[1,1,128]{2,1,0:T(1,128)}, u32[]{:S(2)}) copy-start(s32[1,1,128]{2,1,0:T(1,128)} %rid_ref.1) | copy-start | bytes 1540

commit v6 on v5

--- a/solution.py
+++ b/solution.py
@@ -106,7 +106,7 @@
                   cv_ref, cb_ref, rv_ref, rb_ref, wc, last, send, recv, local):
     pairs = ((rv_hbm, rv_ref), (rb_hbm, rb_ref), (cv_hbm, cv_ref), (cb_hbm, cb_ref), (counts_hbm, counts))
     loads = [pltpu.make_async_copy(src, dst, local.at[1 + k]) for k, (src, dst) in enumerate(pairs)]
-    for load in loads:
+    for load in loads[:4]:
         load.start()
     ring = Ring(send, recv)
     y, zl, core, x, zh = ring.y, ring.zl, ring.core, ring.x, ring.zh
@@ -193,6 +193,7 @@
     f_d[2] = pass_on("y-", up, 2)
     c_u[2], c_d[0] = own("y+", 2), own("y-", 0)
     c_z[2] = own("zl", 2)
+    loads[4].start()
 
     r_zu.wait_recv()
     r_fu = rows("zh+", core, x, zd, pl.ds(0, RHALF))
@@ -428,7 +429,7 @@
         for k in slots:
             pack_shard(acc_ref, *wanted[k], pc, k)
 
-    pack(FAR_O, UP_O, DOWN_O)
+    pack(UP_O)
     pr = pr_ref.at[core]
     ring.meet(barrier)
 
@@ -447,8 +448,13 @@
 
     a_z, a_u, a_d = {}, {}, {}
     for c in (0, 1):
-        a_z[2 * c] = raw("zl", FAR_O, 2 * c, 0)
-        a_u[c], a_d[c] = raw("y+", UP_O, c, 1), raw("y-", DOWN_O, c, 2)
+        a_u[c] = raw("y+", UP_O, c, 1)
+    pack(FAR_O)
+    for c in (0, 2):
+        a_z[c] = raw("zl", FAR_O, c, 0)
+    pack(DOWN_O)
+    for c in (0, 1):
+        a_d[c] = raw("y-", DOWN_O, c, 2)
     for c in (1, 3):
         a_z[c] = raw("zl", FAR_O, c, 0)
     b_c = [ring.copy("core", pr_ref.at[1 - core, w], got_core.at[k]) for k, w in enumerate((xf, xu, xd, x))]

time: 82.1 us -> 81.7 us (level); the launches traced: 81.8 us -> 80.5 us
  Pallas kernels: 81.1 us -> 79.8 us
    pallas_call x1, Pallas kernels: 37.3 us -> 30.5 us  [reduce(): pl.pallas_call(reduce_kernel, out_shape=(pltpu.VMEM((DP, (FULL + 1) * L),...]
    pallas_call x1, Pallas kernels: 6.15 us -> 11.7 us  [blocks(): pl.pallas_call(blocks_kernel, out_shape=(pltpu.VMEM((COL_TILES, DP, L), F...]
where the time goes in v6:
time: 81.7 us; the launch traced here: 80.5 us
  Pallas kernels  79.8 us (98%)
    pallas_call x1, Pallas kernels, gather(): pl.pallas_call(gather_kernel, out_shape=(pltpu.VMEM((TILES, L), BF16), pl...  36.5 us
    pallas_call x1, Pallas kernels, reduce(): pl.pallas_call(reduce_kernel, out_shape=(pltpu.VMEM((DP, (FULL + 1) * L),...  30.5 us
    pallas_call x1, Pallas kernels, blocks(): pl.pallas_call(blocks_kernel, out_shape=(pltpu.VMEM((COL_TILES, DP, L), F...  11.7 us

profile of v6, /device:TPU:1, one launch (start us, length us, event | category | flops | bytes accessed | tf_op | source)
XLA Modules:
  0.0 80.5 jit_solution(16655256572751072429)
XLA Ops:
  0.6 0.0 copy-start
  0.6 0.0 copy-start.2
  0.7 0.0 copy-start.1
  0.7 36.5 %gather.1 = (bf16[17664,128]{1,0:T(8,128)(2,1)S(1)}, bf16[2,4,4,304,128]{4,3,2,1,0:T(8,128)(2,1)S(1)}, bf16[2,4,4,128,304]{4,3,2,1,0:T(8,128)(2,1)S(1)}, s32[128...) custom-call(bf16[300,800]{1,0:T(8,128)(2,1)} %bitcast.12, bf16[800]{0:T(1024)(128)(2,1)} %cb_hbm.1, ...), custom_call_target="tpu_custom_call" | custom-call | tf_op jit(solution)/shard_map/gather/pallas_call | solution.py:281
  37.2 0.0 copy-done
  37.2 0.0 copy-done.2
  37.2 0.0 copy-done.1
  37.2 11.7 %blocks.1 = (f32[50,304,128]{2,1,0:T(8,128)S(1)}, f32[32,304,128]{2,1,0:T(8,128)S(1)}) custom-call(s32[8,32]{1,0:T(8,128)S(1)} %copy-done, s32[1,1,128]{2,1,0:T(1,128)S(1)} %copy-done.1, s32[1,1,128]{2,1,0:T(1,128)S(1)} %copy-done.2, s32[128,128,128]{2,1,0:T(8,128)S(1)} %get-tuple-element.18.counts, ...), custom_call_target="tpu_custom_call", output_to_operand_aliasing={{0}: (7, {}), {1}: (8, {})} | custom-call | tf_op jit(solution)/shard_map/blocks/pallas_call | solution.py:401
  48.9 30.5 %reduce.1 = (f32[304,896]{1,0:T(8,128)S(1)}, f32[304,128]{1,0:T(8,128)S(1)}) custom-call(f32[50,304,128]{2,1,0:T(8,128)S(1)} %get-tuple-element.24.acc_ref, f32[2,4,4,304,128]{4,3,2,1,0:T(8,128)S(1)} %bitcast.8), custom_call_target="tpu_custom_call" | custom-call | tf_op jit(solution)/shard_map/reduce/pallas_call | solution.py:596
  79.4 1.1 %outputs.1 = (f32[300,128]{1,0:T(8,128)}, f32[128]{0:T(128)}, f32[300,800]{1,0:T(8,128)}, f32[800]{0:T(1024)}) custom-call(f32[304,896]{1,0:T(8,128)S(1)} %get-tuple-element.26.oc_ref, f32[304,128]{1,0:T(8,128)S(1)} %get-tuple-element.27.or_ref), custom_call_target="tpu_custom_call" | custom-call | tf_op jit(solution)/shard_map/outputs/pallas_call | solution.py:636
Async XLA Ops:
  0.6 36.6 %copy-start = (s32[8,32]{1,0:T(8,128)S(1)}, s32[8,32]{1,0:T(8,128)}, u32[]{:S(2)}) copy-start(s32[8,32]{1,0:T(8,128)} %total_ref.1) | copy-start | bytes 3076
  0.6 36.6 %copy-start.2 = (s32[1,1,128]{2,1,0:T(1,128)S(1)}, s32[1,1,128]{2,1,0:T(1,128)}, u32[]{:S(2)}) copy-start(s32[1,1,128]{2,1,0:T(1,128)} %cid_ref.1) | copy-start | bytes 1540
  0.7 36.6 %copy-start.1 = (s32[1,1,128]{2,1,0:T(1,128)S(1)}, s32[1,1,128]{2,1,0:T(1,128)}, u32[]{:S(2)}) copy-start(s32[1,1,128]{2,1,0:T(1,128)} %rid_ref.1) | copy-start | bytes 1540
